TPU v7x, 32 devices: a whole 2x2x4 slice. The times are simulated.
32 devices in a mesh: dp: 4 (over z), tensor: 8 (over y, x, core).
Axes of the slice: x: 2, y: 2, z: 4, core: 2. Of those that a mesh axis runs over, the one named last changes fastest.
Arguments:
- tokens: bfloat16 [8, 1024, 2048], P('dp', 'tensor'), may hold values from -6 to 6
- lengths: int32 [8], P('dp'), may hold values from 256 to 1024, as said below
- query_weight: bfloat16 [2048, 2048], P(None, 'tensor'), may hold values from -0.125 to 0.125
- key_weight: bfloat16 [2048, 128], replicated, may hold values from -0.125 to 0.125
- value_weight: bfloat16 [2048, 128], replicated, may hold values from -0.125 to 0.125
- output_weight: bfloat16 [2048, 2048], P('tensor'), may hold values from -2 to 2
- gate_weight: bfloat16 [2048, 5632], P(None, 'tensor'), may hold values from -0.125 to 0.125
- up_weight: bfloat16 [2048, 5632], P(None, 'tensor'), may hold values from -0.125 to 0.125
- down_weight: bfloat16 [5632, 2048], P('tensor'), may hold values from -0.078125 to 0.078125
- gain_attn: bfloat16 [2048], replicated, may hold values from 0.5 to 1.5
- gain_mlp: bfloat16 [2048], replicated, may hold values from 0.5 to 1.5
- pair_grad: float32 [4, 8, 2048, 256], P('dp', 'tensor'), may hold values from -240 to 240
- cotangent: bfloat16 [8, 1024, 2048], P('dp', 'tensor'), may hold values from -6 to 6
Outputs:
- output: bfloat16 [8, 1024, 2048], P('dp', 'tensor')
- grad_tokens: float32 [8, 1024, 2048], P('dp', 'tensor')
- grad_query: float32 [2048, 2048], P(None, 'tensor')
- grad_key: float32 [2048, 128], replicated
- grad_value: float32 [2048, 128], replicated
- output_weight_gradient: float32 [2048, 2048], P('tensor')
- grad_gate: float32 [2048, 5632], P(None, 'tensor')
- grad_up: float32 [2048, 5632], P(None, 'tensor')
- down_weight_gradient: float32 [5632, 2048], P('tensor')
- grad_gain_attn: float32 [2048], replicated
- grad_gain_mlp: float32 [2048], replicated
Inputs may be any that keep to these rules, and one draw needn't show every extreme that they name: `lengths`: in every draw at least one sequence fills its whole slot of 1024 positions.
All inputs are finite; a program needn't handle non-finite values.
Results may differ from a plain program's by a relative error of at most 0.013.
Values may be sent and summed in bfloat16 or wider, within the bound.
No kernel may reach another device: no remote copies, remote signals or barrier semaphores. Data moves between devices by JAX's collectives and lax.ppermute only.
A program may use at most 256 MiB of HBM per device.

v0:
```python
import jax
import jax.numpy as jnp
from jax import lax
from jax.sharding import PartitionSpec as P

HEAD = 128
ATT_BLOCK = 512


SMALL_SHIFT = 1e-05
ROPE_BASE = 10000.0
NEG_FILL = -1e30


def rms_scale(values):
    return lax.rsqrt(jnp.mean(values * values, axis=-1, keepdims=True) + SMALL_SHIFT)


def normed(values, gain_vec):
    return values * rms_scale(values) * gain_vec


def norm_back(values, gain_vec, grad_vals):
    scale_vals = rms_scale(values)
    probability_scaled = grad_vals * gain_vec
    inner_mean = jnp.mean(probability_scaled * values, axis=-1, keepdims=True)
    grad_values = (
        scale_vals * probability_scaled
        - values * (scale_vals * scale_vals * scale_vals) * inner_mean
    )
    grad_gain = jnp.sum(grad_vals * values * scale_vals, axis=(0, 1))
    return (grad_values, grad_gain)


def rope_tables(span_len, head_width):
    half_width = head_width // 2
    frequency = ROPE_BASE ** (-2.0 * jnp.arange(half_width, dtype=jnp.float32) / head_width)
    angles = jnp.arange(span_len, dtype=jnp.float32)[:, None] * frequency[None, :]
    angles = jnp.concatenate([angles, angles], axis=1)
    return (jnp.cos(angles), jnp.sin(angles))


def rotate(values, cosine, sine_tab):
    half_width = values.shape[-1] // 2
    turned = jnp.concatenate([-values[..., half_width:], values[..., :half_width]], axis=-1)
    return values * cosine + turned * sine_tab


def unrotate(grad_vals, cosine, sine_tab):
    half_width = grad_vals.shape[-1] // 2
    scaled = grad_vals * sine_tab
    turned = jnp.concatenate([scaled[..., half_width:], -scaled[..., :half_width]], axis=-1)
    return grad_vals * cosine + turned


def block_scores(query_rows, key_rows, row_start, seq_len):
    head_width = query_rows.shape[-1]
    scores = jnp.einsum(
        "qhc,kc->hqk", query_rows, key_rows, preferred_element_type=jnp.float32
    ) * head_width ** (-0.5)
    query_pos = row_start + jnp.arange(query_rows.shape[0])
    key_pos = jnp.arange(key_rows.shape[0])
    allowed = (key_pos[None, :] <= query_pos[:, None]) & (key_pos[None, :] < seq_len)
    return (scores, allowed[None])


def block_forward(query_rows, key_rows, value_rows, row_start, seq_len):
    scores, allowed = block_scores(query_rows, key_rows, row_start, seq_len)
    masked = jnp.where(allowed, scores, NEG_FILL)
    top_score = jnp.max(masked, axis=-1, keepdims=True)
    exp_terms = jnp.exp(masked - top_score)
    row_totals = jnp.sum(exp_terms, axis=-1, keepdims=True)
    prob_low = (exp_terms / row_totals).astype(jnp.bfloat16)
    mixed_rows = jnp.einsum("hqk,kc->qhc", prob_low, value_rows, preferred_element_type=jnp.float32)
    log_total = (top_score + jnp.log(row_totals))[..., 0]
    return (mixed_rows.astype(jnp.bfloat16), log_total)


def block_backward(query_rows, key_rows, value_rows, grad_rows, total_rows, row_start, seq_len):
    scores, allowed = block_scores(query_rows, key_rows, row_start, seq_len)
    probs_full = jnp.where(allowed, jnp.exp(scores - total_rows[..., None]), 0.0)
    grad_probs = jnp.einsum(
        "qhc,kc->hqk", grad_rows, value_rows, preferred_element_type=jnp.float32
    )
    row_dots = jnp.sum(probs_full * grad_probs, axis=-1, keepdims=True)
    grad_scores = (probs_full * (grad_probs - row_dots)).astype(jnp.bfloat16)
    scale_factor = query_rows.shape[-1] ** (-0.5)
    grad_query = (
        jnp.einsum("hqk,kc->qhc", grad_scores, key_rows, preferred_element_type=jnp.float32)
        * scale_factor
    )
    grad_keys = (
        jnp.einsum("hqk,qhc->kc", grad_scores, query_rows, preferred_element_type=jnp.float32)
        * scale_factor
    )
    grad_values = jnp.einsum(
        "hqk,qhc->kc",
        probs_full.astype(jnp.bfloat16),
        grad_rows,
        preferred_element_type=jnp.float32,
    )
    return (grad_query, grad_keys, grad_values)


def sequence_forward(query_seq, key_seq, value_seq, seq_len):
    span_len, head_count, head_width = query_seq.shape
    blended_pieces = []
    total_parts = []
    for row_start in range(0, span_len, ATT_BLOCK):
        row_stop = row_start + ATT_BLOCK
        operands = (query_seq[row_start:row_stop], key_seq[:row_stop], value_seq[:row_stop])

        def compute(parts_in, row_start=row_start):
            return block_forward(parts_in[0], parts_in[1], parts_in[2], row_start, seq_len)

        result_pair = compute(operands)
        blended_pieces.append(result_pair[0])
        total_parts.append(result_pair[1])
    return (jnp.concatenate(blended_pieces, axis=0), jnp.concatenate(total_parts, axis=1))


def sequence_backward(query_seq, key_seq, value_seq, grad_seq, total_seq, seq_len):
    span_len, head_count, head_width = query_seq.shape
    grad_query_parts = []
    grad_keys = jnp.zeros((span_len, head_width), jnp.float32)
    grad_values = jnp.zeros((span_len, head_width), jnp.float32)
    for row_start in range(0, span_len, ATT_BLOCK):
        row_stop = row_start + ATT_BLOCK
        operands = (
            query_seq[row_start:row_stop],
            key_seq[:row_stop],
            value_seq[:row_stop],
            grad_seq[row_start:row_stop],
            total_seq[:, row_start:row_stop],
        )

        def compute(parts_in, row_start=row_start):
            return block_backward(
                parts_in[0], parts_in[1], parts_in[2], parts_in[3], parts_in[4], row_start, seq_len
            )

        result_set = compute(operands)
        grad_query_parts.append(result_set[0])
        grad_keys = grad_keys.at[:row_stop].add(result_set[1])
        grad_values = grad_values.at[:row_stop].add(result_set[2])
    return (jnp.concatenate(grad_query_parts, axis=0), grad_keys, grad_values)


def per_device(
    tokens,
    lengths,
    query_weight,
    key_weight,
    value_weight,
    output_weight,
    gate_weight,
    up_weight,
    down_weight,
    gain_attn,
    gain_mlp,
    pair_grad,
    cotangent,
):
    seq_count, shard_len, model_width = tokens.shape
    span_len = shard_len * lax.axis_size("tensor")
    head_count = query_weight.shape[1] // HEAD
    row_offset = lax.axis_index("tensor") * shard_len
    local_pos = row_offset + jnp.arange(shard_len)
    local_valid = (local_pos[None, :] < lengths[:, None]).astype(jnp.float32)[..., None]
    cosine, sine_tab = rope_tables(span_len, HEAD)
    token_vector_list = tokens.astype(jnp.float32)
    attn_gain = gain_attn.astype(jnp.float32)
    mlp_gain = gain_mlp.astype(jnp.float32)
    normalized_input = normed(token_vector_list, attn_gain).astype(jnp.bfloat16)
    collected_input = lax.all_gather(normalized_input, "tensor", axis=1, tiled=True)
    unrotated_query = jnp.einsum(
        "wav,vh->wah", collected_input, query_weight, preferred_element_type=jnp.float32
    )
    shared_head_weight = jnp.concatenate([key_weight, value_weight], axis=1)
    shared_head_unrotated = jnp.einsum(
        "wav,vh->wah", collected_input, shared_head_weight, preferred_element_type=jnp.float32
    )
    query_heads = rotate(
        unrotated_query.reshape(seq_count, span_len, head_count, HEAD),
        cosine[:, None, :],
        sine_tab[:, None, :],
    ).astype(jnp.bfloat16)
    key_rows = rotate(shared_head_unrotated[..., :HEAD], cosine, sine_tab).astype(jnp.bfloat16)
    value_rows = shared_head_unrotated[..., HEAD:].astype(jnp.bfloat16)

    def forward_one(packed):
        return sequence_forward(packed[0], packed[1], packed[2], packed[3])

    merged_channel_matrix, log_totals = lax.map(
        forward_one, (query_heads, key_rows, value_rows, lengths)
    )
    merged_channel_matrix = merged_channel_matrix.reshape(seq_count, span_len, head_count * HEAD)
    attention_portion = jnp.einsum(
        "ago,ok->agk", merged_channel_matrix, output_weight, preferred_element_type=jnp.float32
    )
    all_valid = (jnp.arange(span_len)[None, :] < lengths[:, None]).astype(jnp.float32)[..., None]
    placed = jnp.zeros((seq_count, span_len, model_width), jnp.float32)
    placed = lax.dynamic_update_slice_in_dim(placed, token_vector_list, row_offset, 1)
    hidden_all = lax.psum(all_valid * attention_portion + placed, "tensor")
    hidden = lax.dynamic_slice_in_dim(hidden_all, row_offset, shard_len, 1)
    collected_middle = normed(hidden_all, mlp_gain).astype(jnp.bfloat16)
    gate_entries = jnp.einsum(
        "kcj,jr->kcr", collected_middle, gate_weight, preferred_element_type=jnp.float32
    )
    up_entries = jnp.einsum(
        "kcj,jr->kcr", collected_middle, up_weight, preferred_element_type=jnp.float32
    )
    activation_entries, pull_act = jax.vjp(
        lambda gate_in, up_in: jax.nn.silu(gate_in) * up_in, gate_entries, up_entries
    )
    activation_lowered = activation_entries.astype(jnp.bfloat16)
    feedforward_portion = jnp.einsum(
        "aeo,ok->aek", activation_lowered, down_weight, preferred_element_type=jnp.float32
    )
    mlp_rows = lax.psum_scatter(feedforward_portion, "tensor", scatter_dimension=1, tiled=True)
    output = (hidden + local_valid * mlp_rows).astype(jnp.bfloat16)
    grad_y = cotangent.astype(jnp.float32)
    feedforward_gradient = lax.all_gather(
        (local_valid * grad_y).astype(jnp.bfloat16), "tensor", axis=1, tiled=True
    )
    down_weight_gradient = jnp.einsum(
        "cpk,cpr->kr", activation_lowered, feedforward_gradient, preferred_element_type=jnp.float32
    )
    activation_gradient = jnp.einsum(
        "rtb,zb->rtz", feedforward_gradient, down_weight, preferred_element_type=jnp.float32
    )
    grad_gate_vals, grad_up_vals = pull_act(activation_gradient)
    gate_gradient_lowered = grad_gate_vals.astype(jnp.bfloat16)
    up_gradient_lowered = grad_up_vals.astype(jnp.bfloat16)
    grad_gate = jnp.einsum(
        "mop,mox->px", collected_middle, gate_gradient_lowered, preferred_element_type=jnp.float32
    )
    grad_up = jnp.einsum(
        "mop,mox->px", collected_middle, up_gradient_lowered, preferred_element_type=jnp.float32
    )
    middle_portion = jnp.einsum(
        "aio,zo->aiz", gate_gradient_lowered, gate_weight, preferred_element_type=jnp.float32
    )
    middle_portion = middle_portion + jnp.einsum(
        "aio,zo->aiz", up_gradient_lowered, up_weight, preferred_element_type=jnp.float32
    )
    grad_mid = lax.psum_scatter(middle_portion, "tensor", scatter_dimension=1, tiled=True)
    grad_hidden_norm, mlp_gain_part = norm_back(hidden, mlp_gain, grad_mid)
    latent_state_slope = grad_y + grad_hidden_norm
    mixing_layer_slope = lax.all_gather(
        (local_valid * latent_state_slope).astype(jnp.bfloat16), "tensor", axis=1, tiled=True
    )
    output_weight_gradient = jnp.einsum(
        "ytx,ytc->xc", merged_channel_matrix, mixing_layer_slope, preferred_element_type=jnp.float32
    )
    grad_mixed = jnp.einsum(
        "xfa,oa->xfo", mixing_layer_slope, output_weight, preferred_element_type=jnp.float32
    ).astype(jnp.bfloat16)
    grad_mixed = grad_mixed.reshape(seq_count, span_len, head_count, HEAD)

    def backward_one(packed):
        return sequence_backward(packed[0], packed[1], packed[2], packed[3], packed[4], packed[5])

    grad_q_heads, grad_k_sum, grad_v_sum = lax.map(
        backward_one, (query_heads, key_rows, value_rows, grad_mixed, log_totals, lengths)
    )
    unrotated_query_gradient = (
        unrotate(grad_q_heads, cosine[:, None, :], sine_tab[:, None, :])
        .reshape(seq_count, span_len, head_count * HEAD)
        .astype(jnp.bfloat16)
    )
    shared_head_gradient = jnp.concatenate(
        [unrotate(grad_k_sum, cosine, sine_tab), grad_v_sum], axis=-1
    ).astype(jnp.bfloat16)
    grad_query = jnp.einsum(
        "gob,gow->bw", collected_input, unrotated_query_gradient, preferred_element_type=jnp.float32
    )
    shared_head_portion = jnp.einsum(
        "gob,gow->bw", collected_input, shared_head_gradient, preferred_element_type=jnp.float32
    )
    input_portion = jnp.einsum(
        "ezi,pi->ezp", unrotated_query_gradient, query_weight, preferred_element_type=jnp.float32
    )
    input_portion = input_portion + jnp.einsum(
        "ezi,pi->ezp", shared_head_gradient, shared_head_weight, preferred_element_type=jnp.float32
    )
    grad_in = lax.psum_scatter(input_portion, "tensor", scatter_dimension=1, tiled=True)
    grad_x_norm, attn_gain_part = norm_back(token_vector_list, attn_gain, grad_in)
    grad_tokens = latent_state_slope + grad_x_norm
    shared = lax.psum(
        (shared_head_portion + pair_grad[0, 0], attn_gain_part, mlp_gain_part), ("dp", "tensor")
    )
    summed = lax.psum(
        (grad_query, output_weight_gradient, grad_gate, grad_up, down_weight_gradient), "dp"
    )
    return (
        output,
        grad_tokens,
        summed[0],
        shared[0][:, :HEAD],
        shared[0][:, HEAD:],
        summed[1],
        summed[2],
        summed[3],
        summed[4],
        shared[1],
        shared[2],
    )


def solution(mesh):
    placed = (
        P("dp", "tensor", None),
        P("dp"),
        P(None, "tensor"),
        P(),
        P(),
        P("tensor", None),
        P(None, "tensor"),
        P(None, "tensor"),
        P("tensor", None),
        P(),
        P(),
        P("dp", "tensor", None, None),
        P("dp", "tensor", None),
    )
    return jax.shard_map(
        per_device,
        mesh=mesh,
        in_specs=placed,
        out_specs=(
            P("dp", "tensor", None),
            P("dp", "tensor", None),
            P(None, "tensor"),
            P(),
            P(),
            P("tensor", None),
            P(None, "tensor"),
            P(None, "tensor"),
            P("tensor", None),
            P(),
            P(),
        ),
        check_vma=False,
    )
```

profile of v0, /device:TPU:0, one launch (start us, length us, event | category | flops | bytes accessed | tf_op | source)
XLA Modules:
  0.0 1803.5 jit_solution(9439564690698481791)
XLA Ops:
  19.7 50.8 %all-gather.4.cloned.1.call-done = bf16[2,1024,2048]{2,1,0:T(8,128)(2,1)} async-done(((bf16[2,128,2048]{2,1,0:T(8,128)(2,1)}), bf16[2,1024,2048]{2,1,0:T(8,128)(2,1)}) %all-gather.4.cloned.1.call-update) | async-done | bytes 8388624 | tf_op jit(solution)/shard_map/all_gather | solution.py:175
  91.8 21.0 %while.35 = (s32[]{:T(128)}, bf16[2,1024,2,128]{1,3,2,0:T(8,128)(2,1)}, f32[2,2,1024]{2,1,0:T(2,128)S(1)}, bf16[2,1024,128]{1,2,0:T(8,128)(2,1)S(1)}, s32[2]{0:T...) while((s32[]{:T(128)}, ...), condition=%wide.region_6.7_spmd, body=%wide.region_1.6_spmd.sunk | while | flops 824969216 | bytes 32859860 | solution.py:194
  112.8 9.8 broadcast_multiply_fusion
  128.6 215.3 %all-reduce.8.cloned.1.call-done = f32[2,1024,2048]{2,1,0:T(8,128)} async-done(((f32[2,1024,2048]{2,1,0:T(8,128)}), f32[2,1024,2048]{2,1,0:T(8,128)}) %all-reduce.8.cloned.1.call-update) | async-done | bytes 16777232 | tf_op jit(solution)/shard_map/psum | solution.py:204
  358.8 8.0 fusion.85
  366.8 8.0 fusion.89
  374.8 26.2 %all-gather.6.cloned.1.call-done = bf16[2,1024,2048]{2,1,0:T(8,128)(2,1)} async-done(((bf16[2,128,2048]{2,1,0:T(8,128)(2,1)}), bf16[2,1024,2048]{2,1,0:T(8,128)(2,1)}) %all-gather.6.cloned.1.call-update) | async-done | bytes 8388624 | tf_op jit(solution)/shard_map/all_gather | solution.py:223
  401.0 14.7 multiply_convert_fusion.1
  415.8 10.7 fusion.87
  426.5 13.8 convolution_add_fusion.1
  440.3 13.7 fusion.82
  456.4 100.0 %reduce-scatter.6.cloned.1.call-done = f32[2,128,2048]{2,1,0:T(8,128)} async-done(((f32[2,1024,2048]{2,1,0:T(8,128)}), f32[2,128,2048]{2,1,0:T(8,128)}) %reduce-scatter.6.cloned.1.call-update) | async-done | bytes 2097168 | tf_op jit(solution)/shard_map/reduce_scatter | solution.py:247
  560.0 116.3 %reduce-scatter.4.cloned.1.call-done = f32[2,128,2048]{2,1,0:T(8,128)} async-done(((f32[2,1024,2048]{2,1,0:T(8,128)}), f32[2,128,2048]{2,1,0:T(8,128)}) %reduce-scatter.4.cloned.1.call-update) | async-done | bytes 2097168 | tf_op jit(solution)/shard_map/reduce_scatter | solution.py:220
  681.3 54.3 %all-gather.8.cloned.1.call-done = bf16[2,1024,2048]{2,1,0:T(8,128)(2,1)} async-done(((bf16[2,128,2048]{2,1,0:T(8,128)(2,1)}), bf16[2,1024,2048]{2,1,0:T(8,128)(2,1)}) %all-gather.8.cloned.1.call-update) | async-done | bytes 8388624 | tf_op jit(solution)/shard_map/all_gather | solution.py:250
  742.5 49.3 %while.36 = (s32[]{:T(128)}, f32[2,1024,2,128]{1,3,2,0:T(8,128)}, f32[2,1024,128]{1,2,0:T(8,128)}, bf16[2,1024,128]{1,2,0:T(8,128)(2,1)}, bf16[2,1024,128]{2,1,0...) while((s32[]{:T(128)}, f32[2,1024,2,128]{1,3,2,0:T(8,128)}, ...), condition=%wide.region_16.17_spmd, body=%wide.region_13.16_spmd.sunk | while | flops 2036400128 | bytes 108604856 | solution.py:264
  807.6 8.3 fusion.111
  815.9 14.2 convolution_add_fusion
  831.9 10.5 convolution_bitcast_fusion.3
  842.4 10.2 convolution_bitcast_fusion.4
  852.7 10.2 convolution_bitcast_fusion.5
  870.6 66.2 %all-reduce.10.cloned.1.call-done = f32[2048,256]{1,0:T(8,128)} async-done(((f32[2048,256]{1,0:T(8,128)}), f32[2048,256]{1,0:T(8,128)}) %all-reduce.10.cloned.1.call-update) | async-done | bytes 2097168 | tf_op jit(solution)/shard_map/psum | solution.py:290
  939.8 115.5 %reduce-scatter.8.cloned.1.call-done = f32[2,128,2048]{2,1,0:T(8,128)} async-done(((f32[2,1024,2048]{2,1,0:T(8,128)}), f32[2,128,2048]{2,1,0:T(8,128)}) %reduce-scatter.8.cloned.1.call-update) | async-done | bytes 2097168 | tf_op jit(solution)/shard_map/reduce_scatter | solution.py:287
  1057.4 45.1 %all-reduce.2 = (f32[2048]{0:T(1024)}, f32[2048]{0:T(1024)}) all-reduce(f32[2048]{0:T(1024)S(1)} %get-tuple-element.302, f32[2048]{0:T(1024)S(1)} %copy-done.42), channel_id=1, replica_groups=mesh['dp'=4,'tensor'=8] {'dp','tensor'}, use_global_device_ids=true, to_apply=%region_26.27 | all-reduce | flops 4096 | bytes 32768 | tf_op jit(solution)/shard_map/psum | solution.py:290
  1108.0 670.9 %all-reduce.12.cloned.1.call-done = (f32[2048,256]{1,0:T(8,128)}, f32[256,2048]{1,0:T(8,128)}, f32[2048,704]{0,1:T(8,128)}, f32[2048,704]{0,1:T(8,128)}, f32[704,2048]{1,0:T(8,128)}) async-done(((f32[2048,256]{1,0:T(8,128)}, f32[256,2048]{1,0:T(8,128)}, f32[2048,704]{0,1:T(8,128)}, f32[2048,704]{0,1:T(8,128)}, f32[704,2048]{1,0:T(8,128)}), (f32[2048,256]{1,0:T(8,128)}, f32[256,2048]{1,0:T(8,128)}, ...) | async-done | bytes 21495824 | tf_op jit(solution)/shard_map/psum | solution.py:293
  (325 shorter events, 194.8 us)
Async XLA Ops:
  7.2 393.8 %copy-start = (bf16[704,2048]{1,0:T(8,128)(2,1)S(1)}, bf16[704,2048]{1,0:T(8,128)(2,1)}, u32[]{:S(2)}) copy-start(bf16[704,2048]{1,0:T(8,128)(2,1)} %param.37) | copy-start | bytes 8650756
  7.2 63.4 %all-gather.4.cloned.1.call-start = ((), (), s32[]{:S(2)}) async-start(), calls=%async_computation.3 | async-start | bytes 9437184 | tf_op jit(solution)/shard_map/all_gather | solution.py:175
  13.3 330.6 %all-reduce.8.cloned.1.call-start = ((), (), s32[]{:S(2)}) async-start(), calls=%async_computation.4 | async-start | bytes 33554432 | tf_op jit(solution)/shard_map/psum | solution.py:204
  125.9 275.1 %all-gather.6.cloned.1.call-start = ((), (), s32[]{:S(2)}) async-start(), calls=%async_computation.6 | async-start | bytes 9437184 | tf_op jit(solution)/shard_map/all_gather | solution.py:223
  128.5 427.9 %reduce-scatter.6.cloned.1.call-start = ((), (), s32[]{:S(2)}) async-start(), calls=%async_computation.7 | async-start | bytes 18874368 | tf_op jit(solution)/shard_map/reduce_scatter | solution.py:247
  128.6 547.7 %copy-start.36 = (f32[2048]{0:T(1024)}, f32[2048]{0:T(1024)S(1)}, u32[]{:S(2)}) copy-start(f32[2048]{0:T(1024)S(1)} %convert_element_type.120) | copy-start | bytes 24580
  440.3 236.0 %reduce-scatter.4.cloned.1.call-start = ((), (), s32[]{:S(2)}) async-start(), calls=%async_computation.5 | async-start | bytes 18874368 | tf_op jit(solution)/shard_map/reduce_scatter | solution.py:220
  454.1 281.5 %all-gather.8.cloned.1.call-start = ((), (), s32[]{:S(2)}) async-start(), calls=%async_computation.8 | async-start | bytes 9437184 | tf_op jit(solution)/shard_map/all_gather | solution.py:250
  456.4 224.6 %copy-start.45 = (f32[2,128]{1,0:T(2,128)}, f32[2,128]{1,0:T(2,128)S(1)}, u32[]{:S(2)}) copy-start(f32[2,128]{1,0:T(2,128)S(1)} %get-tuple-element.377) | copy-start | bytes 3076
  456.4 224.6 %copy-start.47 = (f32[2,128]{1,0:T(2,128)}, f32[2,128]{1,0:T(2,128)S(1)}, u32[]{:S(2)}) copy-start(f32[2,128]{1,0:T(2,128)S(1)} %get-tuple-element.376) | copy-start | bytes 3076
  560.0 121.1 %copy-start.49 = (f32[2,128]{1,0:T(2,128)}, f32[2,128]{1,0:T(2,128)S(1)}, u32[]{:S(2)}) copy-start(f32[2,128]{1,0:T(2,128)S(1)} %broadcast_multiply_fusion.4) | copy-start | bytes 3076
  681.0 255.8 %all-reduce.10.cloned.1.call-start = ((), (), s32[]{:S(2)}) async-start(), calls=%async_computation.10 | async-start | bytes 4194304 | tf_op jit(solution)/shard_map/psum | solution.py:290
  802.9 252.4 %reduce-scatter.8.cloned.1.call-start = ((), (), s32[]{:S(2)}) async-start(), calls=%async_computation.9 | async-start | bytes 18874368 | tf_op jit(solution)/shard_map/reduce_scatter | solution.py:287
  830.1 948.8 %all-reduce.12.cloned.1.call-start = ((), (), s32[]{:S(2)}) async-start(), calls=%async_computation.11 | async-start | bytes 42991616 | tf_op jit(solution)/shard_map/psum | solution.py:293
  870.5 184.8 %copy-start.6 = (bf16[2,128,2048]{2,1,0:T(8,128)(2,1)S(1)}, bf16[2,128,2048]{2,1,0:T(8,128)(2,1)}, u32[]{:S(2)}) copy-start(bf16[2,128,2048]{2,1,0:T(8,128)(2,1)} %param.29) | copy-start | bytes 3145732
  870.5 184.8 %copy-start.39 = (f32[2048]{0:T(1024)S(1)}, f32[2048]{0:T(1024)}, u32[]{:S(2)}) copy-start(f32[2048]{0:T(1024)} %copy-done.38) | copy-start | bytes 24580
  870.5 184.8 %copy-start.44 = (f32[2,128]{1,0:T(2,128)S(1)}, f32[2,128]{1,0:T(2,128)}, u32[]{:S(2)}) copy-start(f32[2,128]{1,0:T(2,128)} %copy-done.43) | copy-start | bytes 3076
  870.5 186.9 %copy-start.42 = (f32[2048]{0:T(1024)S(1)}, f32[2048]{0:T(1024)}, u32[]{:S(2)}) copy-start(f32[2048]{0:T(1024)} %get-tuple-element.300) | copy-start | bytes 24580
  870.5 232.0 %copy-start.15 = (bf16[2,128,2048]{2,1,0:T(8,128)(2,1)S(1)}, bf16[2,128,2048]{2,1,0:T(8,128)(2,1)}, u32[]{:S(2)}) copy-start(bf16[2,128,2048]{2,1,0:T(8,128)(2,1)} %param.41) | copy-start | bytes 3145732
  870.5 232.0 %copy-start.37 = (f32[2048]{0:T(1024)S(1)}, f32[2048]{0:T(1024)}, u32[]{:S(2)}) copy-start(f32[2048]{0:T(1024)} %copy-done.36) | copy-start | bytes 24580
  870.5 232.0 %copy-start.46 = (f32[2,128]{1,0:T(2,128)S(1)}, f32[2,128]{1,0:T(2,128)}, u32[]{:S(2)}) copy-start(f32[2,128]{1,0:T(2,128)} %copy-done.45) | copy-start | bytes 3076
  870.5 232.0 %copy-start.48 = (f32[2,128]{1,0:T(2,128)S(1)}, f32[2,128]{1,0:T(2,128)}, u32[]{:S(2)}) copy-start(f32[2,128]{1,0:T(2,128)} %copy-done.47) | copy-start | bytes 3076
  870.5 232.0 %copy-start.50 = (f32[2,128]{1,0:T(2,128)S(1)}, f32[2,128]{1,0:T(2,128)}, u32[]{:S(2)}) copy-start(f32[2,128]{1,0:T(2,128)} %copy-done.49) | copy-start | bytes 3076
  870.6 232.0 %copy-start.51 = (f32[2,128]{1,0:T(2,128)S(1)}, f32[2,128]{1,0:T(2,128)}, u32[]{:S(2)}) copy-start(f32[2,128]{1,0:T(2,128)} %get-tuple-element.374) | copy-start | bytes 3076
  (66 other events, 501.5 us)
Sparse Core Ops, SparseCore 0:
  13.4 57.0 all-gather.3
  126.0 217.8 all-reduce.7
  346.6 54.3 all-gather.5
  440.4 115.9 reduce-scatter.5
  560.3 115.9 reduce-scatter.3
  681.2 54.3 all-gather.7
  803.0 133.7 all-reduce.9
  940.4 114.8 reduce-scatter.7
  1059.6 719.2 all-reduce.11
where the time goes:
time: 1810 us; the launch traced here: 1800 us
  waiting for transfers between devices  1420 us (78%)
  matrix products  203 us (11%)
  other arithmetic  71.8 us (4%)
  local copies, waits for them, and re-layouts  51.2 us (3%)
  blocking collectives  45.1 us (2%)
    psum x1, waiting for transfers between devices, per_device(): lax.psum((grad_query, output_weight_gradient, grad_gate, grad_up, down_we...  671 us
    psum x1, waiting for transfers between devices, per_device(): hidden_all = lax.psum(all_valid * attention_portion + placed, 'tensor')  215 us
    reduce_scatter x1, waiting for transfers between devices, per_device(): lax.psum_scatter(feedforward_portion, 'tensor', scatter_dimension=1, tile...  116 us
    reduce_scatter x1, waiting for transfers between devices, per_device(): lax.psum_scatter(input_portion, 'tensor', scatter_dimension=1, tiled=True)  115 us
    reduce_scatter x1, waiting for transfers between devices, per_device(): lax.psum_scatter(middle_portion, 'tensor', scatter_dimension=1, tiled=True)  100 us
    psum x1, waiting for transfers between devices, per_device(): lax.psum((shared_head_portion + pair_grad[0, 0], attn_gain_part, mlp_gain...  66.2 us
    all_gather x1, waiting for transfers between devices, per_device(): lax.all_gather((local_valid * latent_state_slope).astype(jnp.bfloat16), '...  54.3 us
    all_gather x1, waiting for transfers between devices, per_device(): lax.all_gather(normalized_input, 'tensor', axis=1, tiled=True)  50.8 us
  transfers between devices with their start and end apart: 9, of which 9 were waited for; matrix products, arithmetic and copies ran while one was open for 7% of the time, Pallas kernels for 0%

commit v1 on v0

v1 whole, which is shorter than its diff:
```python
import functools

import jax
import jax.numpy as jnp
from jax import lax
from jax.experimental import pallas as pl
from jax.experimental.pallas import tpu as pltpu
from jax.sharding import PartitionSpec as P

HEAD = 128
KEY_BLOCK = 256
SMALL_SHIFT = 1e-05
ROPE_BASE = 10000.0
NEG_FILL = -1e30
LOG2E = 1.4426950408889634
F32 = jnp.float32
BF16 = jnp.bfloat16


def rms_scale(values):
    return lax.rsqrt(jnp.mean(values * values, axis=-1, keepdims=True) + SMALL_SHIFT)


def normed(values, gain_vec):
    return values * rms_scale(values) * gain_vec


def norm_back(values, gain_vec, grad_vals):
    scale_vals = rms_scale(values)
    scaled = grad_vals * gain_vec
    inner_mean = jnp.mean(scaled * values, axis=-1, keepdims=True)
    grad_values = scale_vals * scaled - values * (scale_vals * scale_vals * scale_vals) * inner_mean
    grad_gain = jnp.sum(grad_vals * values * scale_vals, axis=(0, 1))
    return grad_values, grad_gain


def rope_block(start, rows):
    half = HEAD // 2
    frequency = ROPE_BASE ** (-2.0 * jnp.arange(half, dtype=F32) / HEAD)
    angles = (start + jnp.arange(rows)).astype(F32)[:, None] * frequency[None, :]
    cosine, sine = jnp.cos(angles), jnp.sin(angles)
    return jnp.concatenate([cosine, cosine], 1), jnp.concatenate([-sine, sine], 1)


def swap(values, bit):
    n = lax.axis_size("tensor")
    return lax.ppermute(values, "tensor", [(i, i ^ bit) for i in range(n)])


def dot(a, b, dims, out=F32):
    return lax.dot_general(a, b, (dims, ((), ())), preferred_element_type=F32).astype(out)


def add_up(*parts):
    total = parts[0].astype(F32)
    for part in parts[1:]:
        total = total + part.astype(F32)
    return total


def key_branches(start, rows, span, body):
    blocks = span // KEY_BLOCK
    needed = (start + rows + KEY_BLOCK - 1) // KEY_BLOCK
    for count in range(1, blocks + 1):
        pl.when(needed == count)(functools.partial(body, count * KEY_BLOCK))


def stack_heads(values, heads):
    return jnp.concatenate([values[:, h * HEAD : (h + 1) * HEAD] for h in range(heads)], axis=0)


def matmul(a, b, contract):
    return lax.dot_general(a, b, (contract, ((), ())), preferred_element_type=F32)


def masked_scores(keys, query, start, rows, heads, count):
    scores = matmul(keys, query, ((1,), (1,)))
    key_pos = lax.broadcasted_iota(jnp.int32, (KEY_BLOCK, rows), 0) + (count - KEY_BLOCK)
    row_pos = lax.broadcasted_iota(jnp.int32, (KEY_BLOCK, rows), 1) + start
    allowed = key_pos <= row_pos
    last = scores[count - KEY_BLOCK :]
    last = jnp.concatenate(
        [jnp.where(allowed, last[:, h * rows : (h + 1) * rows], NEG_FILL) for h in range(heads)], axis=1
    )
    if count == KEY_BLOCK:
        return last
    return jnp.concatenate([scores[: count - KEY_BLOCK], last], axis=0)


def forward_kernel(
    place, lengths, x0_ref, x1_ref, wq_ref, kv_ref, cos_ref, sin_ref, mixed_ref, query_ref, lse_ref, raw_ref, vt_ref
):
    a = pl.program_id(0)
    seqs, span = kv_ref.shape[0], kv_ref.shape[1]
    rows = x0_ref.shape[0] // seqs
    heads = wq_ref.shape[1] // HEAD
    start = place[a] * rows
    cosine, sine = cos_ref[0], sin_ref[0]
    factor = HEAD ** (-0.5) * LOG2E

    @pl.when(a == 0)
    def _():
        raw_ref[...] = matmul(x0_ref[...], wq_ref[...], ((1,), (0,)))
        for s in range(seqs):
            vt_ref[s] = kv_ref[s, :, HEAD:].T

    @pl.when(a == 1)
    def _():
        raw_ref[...] = matmul(x1_ref[...], wq_ref[...], ((1,), (0,)))

    for s in range(seqs):
        here = slice(s * rows, (s + 1) * rows)
        pieces = []
        for h in range(heads):
            raw = raw_ref[here, h * HEAD : (h + 1) * HEAD]
            pieces.append((raw * cosine + pltpu.roll(raw, HEAD // 2, 1) * sine).astype(BF16))
        query = jnp.concatenate(pieces, axis=0)
        query_ref[0, s] = query
        live = start < lengths[s]

        def body(count, s=s, here=here, query=query):
            scores = masked_scores(kv_ref[s, :count, :HEAD], query, start, rows, heads, count)
            top = jnp.max(scores, axis=0, keepdims=True)
            terms = jnp.exp2((scores - top) * factor)
            total = jnp.sum(terms, axis=0, keepdims=True)
            out = matmul(vt_ref[s, :, :count], terms.astype(BF16), ((1,), (0,))) / total
            lse_ref[0, s] = jnp.broadcast_to(top * factor + jnp.log2(total), lse_ref.shape[2:])
            for h in range(heads):
                piece = out[:, h * rows : (h + 1) * rows].T
                mixed_ref[0, here, h * HEAD : (h + 1) * HEAD] = piece.astype(BF16)

        @pl.when(live)
        def _(body=body):
            key_branches(start, rows, span, body)

        @pl.when(jnp.logical_not(live))
        def _(s=s, here=here):
            mixed_ref[0, here] = jnp.zeros((rows, heads * HEAD), BF16)
            lse_ref[0, s] = jnp.zeros(lse_ref.shape[2:], F32)


def whole(shape):
    return pl.BlockSpec(shape, lambda a, *_: (0,) * len(shape))


def blocked(shape):
    return pl.BlockSpec((1, *shape[1:]), lambda a, *_: (a,) + (0,) * (len(shape) - 1))


def attention_forward(place, lengths, parts, query_weights, kv, cosine, sine):
    flat, width = parts[0].shape
    seqs, span = kv.shape[0], kv.shape[1]
    rows, wide = flat // seqs, query_weights.shape[1]
    heads = wide // HEAD
    shapes = [(2, flat, wide), (2, seqs, heads * rows, HEAD), (2, seqs, 8, heads * rows)]
    return pl.pallas_call(
        forward_kernel,
        grid_spec=pltpu.PrefetchScalarGridSpec(
            num_scalar_prefetch=2,
            grid=(2,),
            in_specs=[
                whole(parts[0].shape),
                whole(parts[1].shape),
                whole(query_weights.shape),
                whole(kv.shape),
                blocked(cosine.shape),
                blocked(sine.shape),
            ],
            out_specs=[blocked(shape) for shape in shapes],
            scratch_shapes=[pltpu.VMEM((flat, wide), F32), pltpu.VMEM((seqs, HEAD, span), BF16)],
        ),
        out_shape=[jax.ShapeDtypeStruct(s, t) for s, t in zip(shapes, (BF16, BF16, F32))],
        compiler_params=pltpu.CompilerParams(vmem_limit_bytes=48 * 1024 * 1024),
        cost_estimate=pl.CostEstimate(flops=flat * wide * span, bytes_accessed=kv.size, transcendentals=0),
        name="attention_forward",
    )(place, lengths, *parts, query_weights, kv, cosine, sine)


def backward_kernel(
    place, lengths, g0_ref, g1_ref, wo_ref, wq_ref, query_ref, lse_ref, kv_ref, cos_ref, sin_ref,
    gq_ref, in_ref, gkv_ref, gm_ref, kt_ref,
):
    a = pl.program_id(0)
    seqs, span = kv_ref.shape[0], kv_ref.shape[1]
    rows = g0_ref.shape[0] // seqs
    heads = wq_ref.shape[1] // HEAD
    start = place[a] * rows
    scale = HEAD ** (-0.5)
    factor = scale * LOG2E

    @pl.when(a == 0)
    def _():
        gm_ref[...] = matmul(g0_ref[...], wo_ref[...], ((1,), (1,))).astype(BF16)
        gkv_ref[...] = jnp.zeros(gkv_ref.shape, F32)
        for s in range(seqs):
            kt_ref[s] = kv_ref[s, :, :HEAD].T

    @pl.when(a == 1)
    def _():
        gm_ref[...] = matmul(g1_ref[...], wo_ref[...], ((1,), (1,))).astype(BF16)

    for s in range(seqs):
        here = slice(s * rows, (s + 1) * rows)
        live = start < lengths[s]

        def body(count, s=s, here=here):
            query = query_ref[0, s]
            grad = stack_heads(gm_ref[here, :], heads)
            scores = masked_scores(kv_ref[s, :count, :HEAD], query, start, rows, heads, count)
            probs = jnp.exp2(scores * factor - lse_ref[0, s, 0:1, :])
            grad_probs = matmul(kv_ref[s, :count, HEAD:], grad, ((1,), (1,)))
            row_dots = jnp.sum(probs * grad_probs, axis=0, keepdims=True)
            grad_scores = (probs * (grad_probs - row_dots)).astype(BF16)
            gkv_ref[s, :count, :HEAD] += scale * matmul(grad_scores, query, ((1,), (0,)))
            gkv_ref[s, :count, HEAD:] += matmul(probs.astype(BF16), grad, ((1,), (0,)))
            grad_query = matmul(kt_ref[s, :, :count], grad_scores, ((1,), (0,)))
            cosine, sine = cos_ref[0], sin_ref[0]
            for h in range(heads):
                piece = grad_query[:, h * rows : (h + 1) * rows].T * scale
                piece = piece * cosine - pltpu.roll(piece, HEAD // 2, 1) * sine
                gq_ref[0, here, h * HEAD : (h + 1) * HEAD] = piece.astype(BF16)

        @pl.when(live)
        def _(body=body):
            key_branches(start, rows, span, body)

        @pl.when(jnp.logical_not(live))
        def _(here=here):
            gq_ref[0, here] = jnp.zeros((rows, heads * HEAD), BF16)

    in_ref[0] = matmul(gq_ref[0], wq_ref[...], ((1,), (1,))).astype(BF16)


def attention_backward(place, lengths, grads, output_weights, query_weights, query, lse, kv, cosine, sine):
    flat, width = grads[0].shape
    seqs, span = kv.shape[0], kv.shape[1]
    wide = query_weights.shape[1]
    operands = (*grads, output_weights, query_weights, query, lse, kv, cosine, sine)
    specs = [whole(v.shape) for v in operands]
    for k in (4, 5, 7, 8):
        specs[k] = blocked(operands[k].shape)
    return pl.pallas_call(
        backward_kernel,
        grid_spec=pltpu.PrefetchScalarGridSpec(
            num_scalar_prefetch=2,
            grid=(2,),
            in_specs=specs,
            out_specs=[blocked((2, flat, wide)), blocked((2, flat, width)), whole(kv.shape)],
            scratch_shapes=[pltpu.VMEM((flat, wide), BF16), pltpu.VMEM((seqs, HEAD, span), BF16)],
        ),
        out_shape=[
            jax.ShapeDtypeStruct((2, flat, wide), BF16),
            jax.ShapeDtypeStruct((2, flat, width), BF16),
            jax.ShapeDtypeStruct(kv.shape, F32),
        ],
        compiler_params=pltpu.CompilerParams(vmem_limit_bytes=56 * 1024 * 1024),
        cost_estimate=pl.CostEstimate(flops=flat * wide * span, bytes_accessed=kv.size, transcendentals=0),
        name="attention_backward",
    )(place, lengths, *operands)


def middle_bits(n):
    bits, bit = [], 2
    while bit < n // 2:
        bits.append(bit)
        bit *= 2
    return bits


def gather_middle(values):
    parts = [values]
    for bit in middle_bits(lax.axis_size("tensor")):
        parts = parts + [swap(part, bit) for part in parts]
    return parts


def reduce_middle(parts):
    for bit in reversed(middle_bits(lax.axis_size("tensor"))):
        half = len(parts) // 2
        parts = [add_up(parts[i], swap(parts[half + i].astype(BF16), bit)) for i in range(half)]
    return parts[0]


def tie(*values):
    return lax.optimization_barrier(values)


class LineSum:
    def __init__(self):
        self.line = lax.axis_size("dp") == 4
        place = lax.axis_index("dp")
        self.outer = (place == 0) | (place == 3)
        self.inward, self.across, self.outward = [], [], []
        self.sums = []

    def advance(self, arrays, others=()):
        if not self.line:
            self.sums += [lax.psum(a, "dp") for a in arrays]
            return others
        arrays, inward, across, outward, others = tie(
            list(arrays), self.inward, self.across, self.outward, others
        )
        self.inward = [(a, lax.ppermute(a, "dp", [(0, 1), (3, 2)])) for a in arrays]
        pairs = [add_up(own, sent).astype(BF16) for own, sent in inward]
        self.across = [(a, lax.ppermute(a, "dp", [(1, 2), (2, 1)])) for a in pairs]
        totals = [add_up(own, sent).astype(BF16) for own, sent in across]
        self.outward = [(a, lax.ppermute(a, "dp", [(1, 0), (2, 3)])) for a in totals]
        self.sums += [jnp.where(self.outer, sent, own) for own, sent in outward]
        return others


def tensor_bits():
    n, bits, bit = lax.axis_size("tensor"), [], 1
    while bit < n:
        bits.append(bit)
        bit *= 2
    return bits


def reduce_blocks(blocks):
    n, me = blocks.shape[0], lax.axis_index("tensor")
    held = [lax.dynamic_index_in_dim(blocks, me ^ r, 0, keepdims=False) for r in range(n)]
    for bit in tensor_bits():
        keep = jnp.stack([held[r] for r in range(len(held)) if r % 2 == 0])
        give = jnp.stack([held[r] for r in range(len(held)) if r % 2 == 1])
        total = add_up(keep, swap(give.astype(BF16), bit))
        held = [total[k] for k in range(total.shape[0])]
    return held[0]


def gather_blocks(block):
    n, me = lax.axis_size("tensor"), lax.axis_index("tensor")
    held = block[None]
    for bit in reversed(tensor_bits()):
        other = swap(held, bit)
        held = jnp.stack([held, other], 1).reshape(2 * held.shape[0], *block.shape)
    result = jnp.zeros_like(held)
    for r in range(n):
        result = lax.dynamic_update_index_in_dim(result, held[r], me ^ r, 0)
    return result


def gather_near(values):
    if lax.axis_size("tensor") != 8:
        return values, values
    return swap(values, 2), swap(values, 4)


def gather_pairs(values):
    parts, bits = [values], tensor_bits()
    for bit in bits:
        parts = parts + [swap(part, bit) for part in parts]
    return [(parts[i], parts[i + 1]) for i in range(0, len(parts), 2)]


def halves(value):
    rows = value.shape[0] // 2
    return value[:rows], value[rows:]


def reduce_begin(count, terms):
    n = lax.axis_size("tensor")
    if n != 8:
        parts = []
        for i in range(count):
            own, other = halves(terms(i, None))
            parts.append(add_up(own, swap(other, 1)))
        while len(parts) > 1:
            half = len(parts) // 2
            parts = [add_up(parts[i], swap(parts[half + i].astype(BF16), 2 * half)) for i in range(half)]
        return parts[0], ()
    own_d, other_d = halves(terms(3, None))
    core_d = swap(other_d, 1)
    own_y, other_y = halves(terms(2, own_d))
    core_y = swap(other_y, 1)
    diagonal = add_up(own_d, core_d).astype(BF16)
    diagonal, own_y = tie(diagonal, own_y)
    first, second = halves(diagonal)
    from_x, from_y = swap(first, 2), swap(second, 4)
    own_x, other_x = halves(terms(1, diagonal))
    core_x = swap(other_x, 1)
    own, other = halves(terms(0, own_x))
    core = swap(other, 1)
    low, high = halves(add_up(own_y, core_y))
    for_y = jnp.concatenate([add_up(low, from_x), high]).astype(BF16)
    low, high = halves(add_up(own_x, core_x))
    for_x = jnp.concatenate([low, add_up(high, from_y)]).astype(BF16)
    return (own, core), (for_x, for_y)


def reduce_end(own, sent):
    if not sent:
        return own
    return add_up(*own, swap(sent[0], 2), swap(sent[1], 4))


def per_device(
    tokens,
    lengths,
    query_weight,
    key_weight,
    value_weight,
    output_weight,
    gate_weight,
    up_weight,
    down_weight,
    gain_attn,
    gain_mlp,
    pair_grad,
    cotangent,
):
    seqs, rows, width = tokens.shape
    n = lax.axis_size("tensor")
    me = lax.axis_index("tensor")
    top = n // 2
    flat = seqs * rows
    local_pos = me * rows + jnp.arange(rows)
    valid = (local_pos[None, :] < lengths[:, None]).astype(F32)[..., None]
    x = tokens.astype(F32)
    attn_gain = gain_attn.astype(F32)
    mlp_gain = gain_mlp.astype(F32)
    grad_y = cotangent.astype(F32)
    kv_weight = jnp.concatenate([key_weight, value_weight], axis=1)

    norm_in = normed(x, attn_gain).astype(BF16).reshape(flat, width)
    far_in = swap(norm_in, top)
    far_in = (far_in, swap(far_in, 1))
    near_in = (norm_in, swap(norm_in, 1))
    query_weights = jnp.concatenate(gather_middle(query_weight), axis=1)
    output_weight, query_weights = tie(output_weight, query_weights)
    output_parts = gather_middle(output_weight)
    heads_width = query_weights.shape[1]
    own_cos, own_sin = rope_block(me * rows, rows)
    kv_raw = dot(norm_in, kv_weight, ((1,), (0,))).reshape(seqs, rows, 2 * HEAD)
    key_raw = kv_raw[..., :HEAD]
    key_own = key_raw * own_cos + jnp.roll(key_raw, HEAD // 2, axis=-1) * own_sin
    kv_own = jnp.concatenate([key_own, kv_raw[..., HEAD:]], axis=-1).astype(BF16)
    kv = lax.all_gather(kv_own, "tensor", axis=1, tiled=True)

    def place_of(offset):
        place = jnp.stack([me ^ offset, me ^ (offset + 1)]).astype(jnp.int32)
        blocks = [rope_block(place[i] * rows, rows) for i in range(2)]
        return place, (jnp.stack([b[0] for b in blocks]), jnp.stack([b[1] for b in blocks]))

    def attend(part, place, table):
        return attention_forward(place, lengths, part, query_weights, kv, *table)

    def portions_of(mixed):
        return [dot(mixed[i], output_weights, ((1,), (0,)), BF16) for i in range(2)]

    near_place, near_table = place_of(0)
    far_place, far_table = place_of(top)
    grad_out = (valid * grad_y).astype(BF16).reshape(flat, width)
    grad_out, _ = tie(grad_out, norm_in)
    grad_far = swap(grad_out, top)
    near_result = attend(near_in, near_place, near_table)
    far_in, _ = tie(far_in, near_result[0])
    far_result = attend(far_in, far_place, far_table)
    output_parts, far_mixed, grad_far = tie(output_parts, far_result[0], grad_far)
    output_weights = jnp.concatenate(output_parts, axis=0)
    far_portions = portions_of(far_mixed)
    for_far = add_up(far_portions[0], swap(far_portions[1], 1)).astype(BF16)
    for_far, near_mixed = tie(for_far, near_result[0])
    from_far = swap(for_far, top)
    near_portions = portions_of(near_mixed)
    near_core = swap(near_portions[1], 1)
    if n == 8:
        grad_out, _ = tie(grad_out, far_mixed)
        grad_parts = [grad_out, swap(grad_out, 2), grad_far, swap(grad_far, 2)]
        from_far, grad_parts = tie(from_far, grad_parts)
        grad_pairs = [(part, swap(part, 1)) for part in grad_parts]
    else:
        grad_pairs = gather_pairs(grad_out)
    grad_chunks = [jnp.concatenate(c) for c in grad_pairs]
    attn_out = add_up(near_portions[0], near_core, from_far)
    hidden = x + valid * attn_out.reshape(seqs, rows, width)

    chips = n // 2
    norm_mid = normed(hidden, mlp_gain).astype(BF16).reshape(flat, width)
    gate_rows, up_rows = gate_weight.T, up_weight.T
    mid_chunks, acts, g_gates, g_ups = [], [], [], []

    def slope_of(i):
        return dot(grad_chunks[i], down_weight, ((1,), (1,)))

    def forward_chunk(pair, slope):
        mid = jnp.concatenate(pair)
        gate = dot(mid, gate_rows, ((1,), (1,)))
        up = dot(mid, up_rows, ((1,), (1,)))
        sig = 1.0 / (1.0 + jnp.exp(-gate))
        silu = gate * sig
        mid_chunks.append(mid)
        acts.append((silu * up).astype(BF16))
        g_gates.append((slope * up * sig * (1.0 + gate * (1.0 - sig))).astype(BF16))
        g_ups.append((slope * silu).astype(BF16))

    if n == 8:
        at_x, at_y = gather_near(norm_mid)
        forward_chunk((norm_mid, swap(norm_mid, 1)), slope_of(0))
        slopes = [slope_of(i) for i in range(1, 4)]
        at_x, at_y, slopes, acts[0] = tie(at_x, at_y, slopes, acts[0])
        size = flat // 2
        diagonal = [swap(at_x[:size], 4), swap(at_y[size:], 2)]
        for i, part in enumerate((at_x, at_y)):
            forward_chunk((part, swap(part, 1)), slopes[i])
        diagonal, acts[1], acts[2] = tie(diagonal, acts[1], acts[2])
        forward_chunk((*diagonal, *[swap(part, 1) for part in diagonal]), slopes[2])
    else:
        for i, pair in enumerate(gather_pairs(norm_mid)):
            forward_chunk(pair, slope_of(i))

    def mid_terms(i, after):
        left, right = g_gates[i], g_ups[i]
        if after is not None:
            left, right, _ = tie(left, right, after)
        terms = dot(left, gate_rows, ((1,), (0,))) + dot(right, up_rows, ((1,), (0,)))
        return terms.astype(BF16)

    sums = LineSum()
    act_all, grad_all = jnp.concatenate(acts), jnp.concatenate(grad_chunks)
    cut = (act_all.shape[1] // 2 + 127) // 128 * 128
    grad_down = dot(act_all[:, :cut], grad_all, ((0,), (0,)), BF16)

    g_gates, g_ups, act_all = sums.advance([grad_down], (g_gates, g_ups, act_all))
    mid_own, mid_sent = reduce_begin(chips, mid_terms)
    grad_rest = dot(act_all[:, cut:], grad_all, ((0,), (0,)), BF16)

    mid_sent, g_gates, g_ups = sums.advance([grad_rest], (mid_sent, g_gates, g_ups))
    mid_all = jnp.concatenate(mid_chunks)
    grad_gate = halves(dot(jnp.concatenate(g_gates), mid_all, ((0,), (0,)), BF16))
    grad_mid = reduce_end(mid_own, mid_sent).reshape(seqs, rows, width)
    back, mlp_gain_part = norm_back(hidden, mlp_gain, grad_mid)
    grad_hidden = grad_y + back
    grad_attn = (valid * grad_hidden).astype(BF16).reshape(flat, width)

    grad_attn, g_ups = sums.advance([grad_gate[0]], (grad_attn, g_ups))
    far_grad = swap(grad_attn, top)
    near_grad = (grad_attn, swap(grad_attn, 1))
    grad_up = halves(dot(jnp.concatenate(g_ups), mid_all, ((0,), (0,)), BF16))

    def attend_back(part, result, place, table):
        return attention_backward(
            place, lengths, part, output_weights, query_weights, result[1], result[2], kv, *table
        )

    def product(left, right):
        return dot(jnp.concatenate(left), jnp.concatenate(right), ((0,), (0,)), BF16)

    far_grad, near_grad = sums.advance([grad_gate[1]], (far_grad, near_grad))
    far_grad = (far_grad, swap(far_grad, 1))
    far_q, far_terms, far_kv = attend_back(far_grad, far_result, far_place, far_table)
    for_far = add_up(far_terms[0], swap(far_terms[1], 1)).astype(BF16)

    for_far, near_grad, far_grad = sums.advance([grad_up[0]], (for_far, near_grad, far_grad))
    from_far = swap(for_far, top)
    unit = output_weight.shape[0]
    mixed = [r[0][i] for r in (near_result, far_result) for i in range(2)]
    wo_full = product(mixed, [*near_grad, *far_grad])
    wo_part = reduce_middle([wo_full[i * unit : (i + 1) * unit] for i in range(heads_width // unit)])
    wo_part = wo_part.astype(BF16)
    near_q, near_terms, near_kv = attend_back(near_grad, near_result, near_place, near_table)
    near_core = swap(near_terms[1], 1)

    from_far, near_terms, near_core, near_q, near_kv, wo_part = sums.advance(
        [grad_up[1]], (from_far, near_terms, near_core, near_q, near_kv, wo_part)
    )
    kv_blocks = (near_kv + far_kv).astype(BF16).reshape(seqs, n, rows, 2 * HEAD).swapaxes(0, 1)
    kv_sum = reduce_blocks(kv_blocks)
    wq_full = product([*near_in, *far_in], [near_q[0], near_q[1], far_q[0], far_q[1]])
    wq_full, kv_sum = tie(wq_full, kv_sum)
    wq_part = reduce_middle([wq_full[:, i * unit : (i + 1) * unit] for i in range(heads_width // unit)])
    wq_part = wq_part.astype(BF16)
    key_grad = kv_sum[..., :HEAD]
    key_grad = key_grad * own_cos - jnp.roll(key_grad, HEAD // 2, axis=-1) * own_sin
    kv_grad = jnp.concatenate([key_grad, kv_sum[..., HEAD:]], -1).astype(BF16).reshape(flat, 2 * HEAD)
    grad_in = add_up(near_terms[0], near_core, from_far)
    grad_in = grad_in + dot(kv_grad, kv_weight, ((1,), (1,)))
    kv_portion = dot(norm_in, kv_grad, ((0,), (0,)))
    back, attn_gain_part = norm_back(x, attn_gain, grad_in.reshape(seqs, rows, width))
    grad_tokens = grad_hidden + back

    kv_portion, attn_gain_part, wq_part, acts = sums.advance(
        [wo_part], (kv_portion, attn_gain_part, wq_part, acts)
    )
    gains = jnp.concatenate([attn_gain_part, mlp_gain_part]).reshape(-1, 2 * HEAD)
    shared = jnp.concatenate([kv_portion + pair_grad[0, 0], gains])
    shared = jnp.pad(shared, ((0, -shared.shape[0] % (16 * n)), (0, 0))).astype(BF16)
    shared = reduce_blocks(shared.reshape(n, -1, 2 * HEAD)).astype(BF16)

    def out_terms(i, after):
        left = acts[i] if after is None else tie(acts[i], after)[0]
        return dot(left, down_weight, ((1,), (0,)), BF16)

    acts, shared = tie(acts, shared)
    out_own, out_sent = reduce_begin(chips, out_terms)

    out_sent = sums.advance([wq_part, shared], out_sent)
    rows_out = reduce_end(out_own, out_sent)
    output = (hidden + valid * rows_out.reshape(seqs, rows, width)).astype(BF16)
    sums.advance([])
    sums.advance([])
    sums.advance([])
    down_1, down_2, gate_1, gate_2, up_1, up_2, wo_sum, wq_sum, shared = sums.sums
    shared = gather_blocks(shared).reshape(-1, 2 * HEAD).astype(F32)
    gains = shared[width : width + gains.shape[0]].reshape(2, width)
    return (
        output,
        grad_tokens,
        wq_sum.astype(F32),
        shared[:width, :HEAD],
        shared[:width, HEAD:],
        wo_sum.astype(F32),
        jnp.concatenate([gate_1, gate_2]).astype(F32).T,
        jnp.concatenate([up_1, up_2]).astype(F32).T,
        jnp.concatenate([down_1, down_2]).astype(F32),
        gains[0],
        gains[1],
    )


def solution(mesh):
    placed = (
        P("dp", "tensor", None),
        P("dp"),
        P(None, "tensor"),
        P(),
        P(),
        P("tensor", None),
        P(None, "tensor"),
        P(None, "tensor"),
        P("tensor", None),
        P(),
        P(),
        P("dp", "tensor", None, None),
        P("dp", "tensor", None),
    )
    return jax.shard_map(
        per_device,
        mesh=mesh,
        in_specs=placed,
        out_specs=(
            P("dp", "tensor", None),
            P("dp", "tensor", None),
            P(None, "tensor"),
            P(),
            P(),
            P("tensor", None),
            P(None, "tensor"),
            P(None, "tensor"),
            P("tensor", None),
            P(),
            P(),
        ),
        check_vma=False,
    )
```

time: 1810 us -> 681 us (0.38)
  waiting for transfers between devices: 1420 us -> 267 us
  starting transfers between devices: 0.54 us -> 113 us
  matrix products: 203 us -> 94.2 us
  Pallas kernels: 0 us -> 45.2 us
  blocking collectives: 45.1 us -> 0 us
    psum x3 -> x0, waiting for transfers between devices: 952 us -> none  [the longest x1 671 us: per_device(): lax.psum((grad_query, output_weight_gradient, grad_gate, grad_up, down_we...]
    reduce_scatter x3 -> x0, waiting for transfers between devices: 332 us -> none  [the longest x1 116 us: per_device(): lax.psum_scatter(feedforward_portion, 'tensor', scatter_dimension=1, tile...]
    ppermute x0 -> x84, waiting for transfers between devices: none -> 267 us  [the longest x57 199 us: swap(): return lax.ppermute(values, 'tensor', [(i, i ^ bit) for i in range(n)])]
    all_gather x3 -> x1, waiting for transfers between devices: 131 us -> 0.01 us  [per_device(): kv = lax.all_gather(kv_own, 'tensor', axis=1, tiled=True)]
    ppermute x0 -> x84, starting transfers between devices: none -> 113 us  [the longest x9 52.6 us: advance(): self.inward = [(a, lax.ppermute(a, 'dp', [(0, 1), (3, 2)])) for a in arrays]]
    dot_general x46 -> x37, matrix products: 203 us -> 94.2 us  [dot(): lax.dot_general(a, b, (dims, ((), ())), preferred_element_type=F32)]
    pallas_call x0 -> x4, Pallas kernels: none -> 45.2 us  [the longest x2 28.5 us: attention_backward(): pl.pallas_call(backward_kernel, grid_spec=pltpu.PrefetchScalarGridSpec(nu...]
    psum x1 -> x0, blocking collectives: 45.1 us -> none  [per_device(): lax.psum((shared_head_portion + pair_grad[0, 0], attn_gain_part, mlp_gain...]
  transfers between devices with their start and end apart: 9 -> 85, of which waited for: 9 -> 30; matrix products, arithmetic and copies ran while one was open for 7% -> 27% of each run, Pallas kernels for 0% -> 7%
where the time goes in v1:
time: 681 us; the launch traced here: 672 us
  waiting for transfers between devices  267 us (39%)
  starting transfers between devices  113 us (17%)
  matrix products  94.2 us (14%)
  other arithmetic  81.5 us (12%)
  local copies, waits for them, and re-layouts  54.2 us (8%)
  Pallas kernels  45.2 us (7%)
  between operations  17 us (2%)
    ppermute x57, waiting for transfers between devices, swap(): return lax.ppermute(values, 'tensor', [(i, i ^ bit) for i in range(n)])  199 us
    dot_general x37, matrix products, dot(): lax.dot_general(a, b, (dims, ((), ())), preferred_element_type=F32)  94.2 us
    ppermute x9, starting transfers between devices, advance(): self.inward = [(a, lax.ppermute(a, 'dp', [(0, 1), (3, 2)])) for a in arrays]  52.6 us
    ppermute x9, waiting for transfers between devices, advance(): lax.ppermute(a, 'dp', [(1, 0), (2, 3)])  47.7 us
    ppermute x57, starting transfers between devices, swap(): return lax.ppermute(values, 'tensor', [(i, i ^ bit) for i in range(n)])  38.5 us
    unnamed x229, local copies, waits for them, and re-layouts  33.6 us
    pallas_call x2, Pallas kernels, attention_backward(): pl.pallas_call(backward_kernel, grid_spec=pltpu.PrefetchScalarGridSpec(nu...  28.5 us
    ppermute x9, waiting for transfers between devices, advance(): self.inward = [(a, lax.ppermute(a, 'dp', [(0, 1), (3, 2)])) for a in arrays]  20.4 us
  transfers between devices with their start and end apart: 85, of which 30 were waited for; matrix products, arithmetic and copies ran while one was open for 27% of the time, Pallas kernels for 7%

profile of v1, /device:TPU:0, one launch (start us, length us, event | category | flops | bytes accessed | tf_op | source)
XLA Modules:
  0.0 672.4 jit_solution(15231381035411509355)
XLA Ops:
  30.1 11.3 %collective-permute-done.2.x0_ref = bf16[256,2048]{1,0:T(8,128)(2,1)} collective-permute-done((bf16[256,2048]{1,0:T(8,128)(2,1)}, bf16[256,2048]{1,0:T(8,128)(2,1)}, u32[]{:S(2)}, u32[]{:S(2)}) %collective-permute-start.2) | collective-permute-done | bytes 1048608 | tf_op jit(solution)/shard_map/ppermute | solution.py:47
  41.4 13.5 %collective-permute-done = bf16[2048,256]{1,0:T(8,128)(2,1)S(1)} collective-permute-done((bf16[2048,256]{1,0:T(8,128)(2,1)}, bf16[2048,256]{1,0:T(8,128)(2,1)S(1)}, u32[]{:S(2)}, u32[]{:S(2)}) %collective-permute-start) | collective-permute-done | bytes 1048608 | tf_op jit(solution)/shard_map/ppermute | solution.py:47
  70.6 9.5 %attention_forward.3 = (bf16[2,256,512]{2,1,0:T(8,128)(2,1)S(1)}, bf16[2,2,512,128]{3,2,1,0:T(8,128)(2,1)S(1)}, f32[2,2,8,512]{3,2,1,0:T(8,128)S(1)}) custom-call(s32[2]{0:T(128)S(1)} %pad_add_fusion.place, s32[2]{0:T(128)S(1)} %copy-done.12, bf16[256,2048]{1,0:T(8,128)(2,1)} %collective-permute-done.2.x0_ref, ...), custom_call_target="tpu_custom_call" | custom-call | flops 134217728 | bytes 524288 | tf_op jit(solution)/shard_map/attention_forward/pallas_call | solution.py:156
  90.4 20.6 %collective-permute-done.9 = bf16[256,2048]{1,0:T(8,128)(2,1)S(1)} collective-permute-done((bf16[256,2048]{1,0:T(8,128)(2,1)}, bf16[256,2048]{1,0:T(8,128)(2,1)S(1)}, u32[]{:S(2)}, u32[]{:S(2)}) %collective-permute-start.9) | collective-permute-done | bytes 1048608 | tf_op jit(solution)/shard_map/ppermute | solution.py:47
  111.0 22.0 %collective-permute-done.10 = bf16[256,2048]{1,0:T(8,128)(2,1)S(1)} collective-permute-done((bf16[256,2048]{1,0:T(8,128)(2,1)}, bf16[256,2048]{1,0:T(8,128)(2,1)S(1)}, u32[]{:S(2)}, u32[]{:S(2)}) %collective-permute-start.10) | collective-permute-done | bytes 1048608 | tf_op jit(solution)/shard_map/ppermute | solution.py:47
  239.4 7.8 %collective-permute-done.29 = bf16[128,2048]{1,0:T(8,128)(2,1)S(1)} collective-permute-done((bf16[128,2048]{1,0:T(8,128)(2,1)S(1)}, bf16[128,2048]{1,0:T(8,128)(2,1)S(1)}, u32[]{:S(2)}, u32[]{:S(2)}) %collective-permute-start.29) | collective-permute-done | bytes 524320 | tf_op jit(solution)/shard_map/ppermute | solution.py:47
  258.1 8.5 %convolution_convert_fusion.1 = bf16[704,2048]{1,0:T(8,128)(2,1)S(1)} fusion(bf16[2048,2048]{1,0:T(8,128)(2,1)} %get-tuple-element.430, bf16[512,704]{0,1:T(8,128)(2,1)S(1)} %get-tuple-element.228, bf16[512,704]{0,1:T(8,128)(2,1)S(1)} %get-tuple-element.227, bf16[512,704]{0,1:T(8,128)(2,1)S(1)} %get-tuple-element.226, ...), kind=kOutput, calls=%fused_computation.29 | convolution fusion | flops 5918556160 | bytes 14155776 | tf_op jit(solution)/shard_map/dot_general | solution.py:51
  268.4 8.7 %collective-permute-done.33 = bf16[256,2048]{1,0:T(8,128)(2,1)S(1)} collective-permute-done((bf16[256,2048]{1,0:T(8,128)(2,1)S(1)}, bf16[256,2048]{1,0:T(8,128)(2,1)S(1)}, u32[]{:S(2)}, u32[]{:S(2)}) %collective-permute-start.33) | collective-permute-done | bytes 1048608 | tf_op jit(solution)/shard_map/ppermute | solution.py:47
  283.9 13.1 %collective-permute-start.35 = (bf16[352,2048]{1,0:T(8,128)(2,1)}, bf16[352,2048]{1,0:T(8,128)(2,1)}, u32[]{:S(2)}, u32[]{:S(2)}) collective-permute-start(bf16[352,2048]{1,0:T(8,128)(2,1)} %get-tuple-element.251), channel_id=1, source_target_pairs={{0,8},{24,16},{1,9},{25,17},{2,10},{26,18},{3,11},{27,19},{4,12},{... | collective-permute-start | bytes 4325384 | tf_op jit(solution)/shard_map/ppermute | solution.py:303
  306.9 22.3 %collective-permute-done.38.g0_ref = bf16[256,2048]{1,0:T(8,128)(2,1)} collective-permute-done((bf16[256,2048]{1,0:T(8,128)(2,1)}, bf16[256,2048]{1,0:T(8,128)(2,1)}, u32[]{:S(2)}, u32[]{:S(2)}) %collective-permute-start.38) | collective-permute-done | bytes 1048608 | tf_op jit(solution)/shard_map/ppermute | solution.py:47
  344.1 7.9 %collective-permute-start.40 = (bf16[352,2048]{1,0:T(8,128)(2,1)S(1)}, bf16[352,2048]{1,0:T(8,128)(2,1)}, u32[]{:S(2)}, u32[]{:S(2)}) collective-permute-start(bf16[352,2048]{1,0:T(8,128)(2,1)S(1)} %copy-done.39), channel_id=1, source_target_pairs={{0,8},{24,16},{1,9},{25,17},{2,10},{26,18},{3,11},{27,19},{4,12},{... | collective-permute-start | bytes 4325384 | tf_op jit(solution)/shard_map/ppermute | solution.py:303
  353.0 15.8 %attention_backward.2 = (bf16[2,256,512]{2,1,0:T(8,128)(2,1)}, bf16[2,256,2048]{2,1,0:T(8,128)(2,1)}, f32[2,1024,256]{2,1,0:T(8,128)}) custom-call(s32[2]{0:T(128)} %copy-done.14, s32[2]{0:T(128)} %lengths.7, bf16[256,2048]{1,0:T(8,128)(2,1)} %collective-permute-done.38.g0_ref, bf16[256,2048]{1,0:T(8,128)(2,1)} %copy-done.61, bf16[512,2048]{1,0:T(8,128)(2,1)} %copy-done.15, ...), custom_call_target="tpu_custom_call" | custom-call | flops 134217728 | bytes 524288 | tf_op jit(solution)/shard_map/attention_backward/pallas_call | solution.py:242
  370.4 8.7 %convolution_convert_fusion = bf16[704,2048]{1,0:T(8,128)(2,1)S(1)} fusion(bf16[2048,2048]{1,0:T(8,128)(2,1)} %get-tuple-element.430, bf16[512,704]{0,1:T(8,128)(2,1)S(1)} %copy-done.69, bf16[512,704]{0,1:T(8,128)(2,1)S(1)} %copy-done.65, bf16[512,704]{0,1:T(8,128)(2,1)S(1)} %copy-done.67, bf16[512,704]{0,1:T(8,128)(2,1)S(1)} %copy-done.104), kind=kOutput, calls=%fused_computation.28 | convolution fusion | flops 5918556160 | bytes 14155776 | tf_op jit(solution)/shard_map/dot_general | solution.py:51
  395.1 7.7 %collective-permute-start.45 = (bf16[352,2048]{1,0:T(8,128)(2,1)}, bf16[352,2048]{1,0:T(8,128)(2,1)}, u32[]{:S(2)}, u32[]{:S(2)}) collective-permute-start(bf16[352,2048]{1,0:T(8,128)(2,1)} %get-tuple-element.278), channel_id=1, source_target_pairs={{0,8},{24,16},{1,9},{25,17},{2,10},{26,18},{3,11},{27,19},{4,12},{... | collective-permute-start | bytes 4325384 | tf_op jit(solution)/shard_map/ppermute | solution.py:303
  402.8 12.8 %attention_backward.3 = (bf16[2,256,512]{2,1,0:T(8,128)(2,1)}, bf16[2,256,2048]{2,1,0:T(8,128)(2,1)}, f32[2,1024,256]{2,1,0:T(8,128)}) custom-call(s32[2]{0:T(128)} %copy-done.13, s32[2]{0:T(128)} %lengths.7, bf16[256,2048]{1,0:T(8,128)(2,1)} %bitcast.22.g0_ref, bf16[256,2048]{1,0:T(8,128)(2,1)} %collective-permute-done.39.g1_ref, ...), custom_call_target="tpu_custom_call" | custom-call | flops 134217728 | bytes 524288 | tf_op jit(solution)/shard_map/attention_backward/pallas_call | solution.py:242
  426.2 18.2 %collective-permute-done.48 = bf16[256,2048]{1,0:T(8,128)(2,1)S(1)} collective-permute-done((bf16[256,2048]{1,0:T(8,128)(2,1)S(1)}, bf16[256,2048]{1,0:T(8,128)(2,1)S(1)}, u32[]{:S(2)}, u32[]{:S(2)}) %collective-permute-start.48) | collective-permute-done | bytes 1048608 | tf_op jit(solution)/shard_map/ppermute | solution.py:47
  452.7 7.6 %collective-permute-start.51 = (bf16[352,2048]{1,0:T(8,128)(2,1)S(1)}, bf16[352,2048]{1,0:T(8,128)(2,1)S(1)}, u32[]{:S(2)}, u32[]{:S(2)}) collective-permute-start(bf16[352,2048]{1,0:T(8,128)(2,1)S(1)} %get-tuple-element.308), channel_id=1, source_target_pairs={{0,8},{24,16},{1,9},{25,17},{2,10},{26,18},{3,11},{27,19},{4,12},{... | collective-permute-start | bytes 4325384 | tf_op jit(solution)/shard_map/ppermute | solution.py:303
  472.4 17.3 %collective-permute-done.57 = bf16[2048,256]{1,0:T(8,128)(2,1)S(1)} collective-permute-done((bf16[2048,256]{1,0:T(8,128)(2,1)S(1)}, bf16[2048,256]{1,0:T(8,128)(2,1)S(1)}, u32[]{:S(2)}, u32[]{:S(2)}) %collective-permute-start.57) | collective-permute-done | bytes 1048608 | tf_op jit(solution)/shard_map/ppermute | solution.py:47
  527.2 10.4 %collective-permute-done.69 = bf16[128,2048]{1,0:T(8,128)(2,1)S(1)} collective-permute-done((bf16[128,2048]{1,0:T(8,128)(2,1)S(1)}, bf16[128,2048]{1,0:T(8,128)(2,1)S(1)}, u32[]{:S(2)}, u32[]{:S(2)}) %collective-permute-start.69) | collective-permute-done | bytes 524320 | tf_op jit(solution)/shard_map/ppermute | solution.py:47
  540.0 11.2 %collective-permute-done.67 = bf16[128,2048]{1,0:T(8,128)(2,1)S(1)} collective-permute-done((bf16[128,2048]{1,0:T(8,128)(2,1)S(1)}, bf16[128,2048]{1,0:T(8,128)(2,1)S(1)}, u32[]{:S(2)}, u32[]{:S(2)}) %collective-permute-start.67) | collective-permute-done | bytes 524320 | tf_op jit(solution)/shard_map/ppermute | solution.py:47
  554.5 8.2 %collective-permute-start.72 = (bf16[2048,256]{1,0:T(8,128)(2,1)S(1)}, bf16[2048,256]{1,0:T(8,128)(2,1)S(1)}, u32[]{:S(2)}, u32[]{:S(2)}) collective-permute-start(bf16[2048,256]{1,0:T(8,128)(2,1)S(1)} %copy-done.42), channel_id=1, source_target_pairs={{0,8},{24,16},{1,9},{25,17},{2,10},{26,18},{3,11},{27,19},{4,12},{... | collective-permute-start | bytes 3145736 | tf_op jit(solution)/shard_map/ppermute | solution.py:303
  567.6 19.0 %collective-permute-done.73 = bf16[272,256]{1,0:T(8,128)(2,1)S(1)} collective-permute-done((bf16[272,256]{1,0:T(8,128)(2,1)S(1)}, bf16[272,256]{1,0:T(8,128)(2,1)S(1)}, u32[]{:S(2)}, u32[]{:S(2)}) %collective-permute-start.73) | collective-permute-done | bytes 139296 | tf_op jit(solution)/shard_map/ppermute | solution.py:303
  596.0 17.4 %collective-permute-done.78 = bf16[256,2048]{1,0:T(8,128)(2,1)S(1)} collective-permute-done((bf16[256,2048]{1,0:T(8,128)(2,1)S(1)}, bf16[256,2048]{1,0:T(8,128)(2,1)S(1)}, u32[]{:S(2)}, u32[]{:S(2)}) %collective-permute-start.78) | collective-permute-done | bytes 1048608 | tf_op jit(solution)/shard_map/ppermute | solution.py:307
  624.4 22.7 %collective-permute-done.80 = bf16[272,256]{1,0:T(8,128)(2,1)S(1)} collective-permute-done((bf16[272,256]{1,0:T(8,128)(2,1)S(1)}, bf16[272,256]{1,0:T(8,128)(2,1)S(1)}, u32[]{:S(2)}, u32[]{:S(2)}) %collective-permute-start.80) | collective-permute-done | bytes 139296 | tf_op jit(solution)/shard_map/ppermute | solution.py:307
  (585 shorter events, 333.3 us)
Async XLA Ops:
  7.2 53.2 %all-gather.2.cloned.1.call-start = ((), (), s32[]{:S(2)}) async-start(), calls=%async_computation | async-start | bytes 1179648 | tf_op jit(solution)/shard_map/all_gather | solution.py:438
  12.7 47.7 %collective-permute-start.4 = (bf16[256,2048]{1,0:T(8,128)(2,1)}, bf16[256,2048]{1,0:T(8,128)(2,1)}, u32[]{:S(2)}, u32[]{:S(2)}) collective-permute-start(bf16[256,2048]{1,0:T(8,128)(2,1)} %bitcast.2.x0_ref), channel_id=1, source_target_pairs={{0,1},{1,0},{2,3},{3,2},{4,5},{5,4},{6,7},{7,6},{8,9},{9,8},{10,11... | collective-permute-start | bytes 3145736 | tf_op jit(solution)/shard_map/ppermute | solution.py:47
  29.2 51.0 %collective-permute-start.5 = (bf16[256,2048]{1,0:T(8,128)(2,1)}, bf16[256,2048]{1,0:T(8,128)(2,1)}, u32[]{:S(2)}, u32[]{:S(2)}) collective-permute-start(bf16[256,2048]{1,0:T(8,128)(2,1)} %bitcast.14), channel_id=1, source_target_pairs={{0,4},{1,5},{2,6},{3,7},{4,0},{5,1},{6,2},{7,3},{8,12},{9,13},{10,... | collective-permute-start | bytes 3145736 | tf_op jit(solution)/shard_map/ppermute | solution.py:47
  86.4 46.7 %collective-permute-start.10 = (bf16[256,2048]{1,0:T(8,128)(2,1)}, bf16[256,2048]{1,0:T(8,128)(2,1)S(1)}, u32[]{:S(2)}, u32[]{:S(2)}) collective-permute-start(bf16[256,2048]{1,0:T(8,128)(2,1)} %collective-permute-done.5), channel_id=1, source_target_pairs={{0,2},{1,3},{2,0},{3,1},{4,6},{5,7},{6,4},{7,5},{8,10},{9,11},{10,... | collective-permute-start | bytes 3145736 | tf_op jit(solution)/shard_map/ppermute | solution.py:47
  88.2 44.8 %collective-permute-start.8 = (bf16[256,2048]{1,0:T(8,128)(2,1)S(1)}, bf16[256,2048]{1,0:T(8,128)(2,1)S(1)}, u32[]{:S(2)}, u32[]{:S(2)}) collective-permute-start(bf16[256,2048]{1,0:T(8,128)(2,1)S(1)} %fusion.38), channel_id=1, source_target_pairs={{0,4},{1,5},{2,6},{3,7},{4,0},{5,1},{6,2},{7,3},{8,12},{9,13},{10,... | collective-permute-start | bytes 3145736 | tf_op jit(solution)/shard_map/ppermute | solution.py:47
  90.3 42.8 %collective-permute-start.7 = (bf16[256,2048]{1,0:T(8,128)(2,1)S(1)}, bf16[256,2048]{1,0:T(8,128)(2,1)S(1)}, u32[]{:S(2)}, u32[]{:S(2)}) collective-permute-start(bf16[256,2048]{1,0:T(8,128)(2,1)S(1)} %convolution_convert_fusion.8), channel_id=1, source_target_pairs={{0,1},{1,0},{2,3},{3,2},{4,5},{5,4},{6,7},{7,6},{8,9},{9,8},{10,11... | collective-permute-start | bytes 3145736 | tf_op jit(solution)/shard_map/ppermute | solution.py:47
  209.2 43.3 %collective-permute-start.24 = (bf16[384,2048]{1,0:T(8,128)(2,1)S(1)}, bf16[384,2048]{1,0:T(8,128)(2,1)S(1)}, u32[]{:S(2)}, u32[]{:S(2)}) collective-permute-start(bf16[384,2048]{1,0:T(8,128)(2,1)S(1)} %convolution_convert_fusion.6), channel_id=1, source_target_pairs={{0,8},{24,16},{1,9},{25,17},{2,10},{26,18},{3,11},{27,19},{4,12},{... | collective-permute-start | bytes 4718600 | tf_op jit(solution)/shard_map/ppermute | solution.py:303
  217.1 51.3 %collective-permute-start.32 = (bf16[256,2048]{1,0:T(8,128)(2,1)S(1)}, bf16[256,2048]{1,0:T(8,128)(2,1)S(1)}, u32[]{:S(2)}, u32[]{:S(2)}) collective-permute-start(bf16[256,2048]{1,0:T(8,128)(2,1)S(1)} %slice.391), channel_id=1, source_target_pairs={{0,1},{1,0},{2,3},{3,2},{4,5},{5,4},{6,7},{7,6},{8,9},{9,8},{10,11... | collective-permute-start | bytes 3145736 | tf_op jit(solution)/shard_map/ppermute | solution.py:47
  283.9 45.3 %collective-permute-start.35 = (bf16[352,2048]{1,0:T(8,128)(2,1)}, bf16[352,2048]{1,0:T(8,128)(2,1)}, u32[]{:S(2)}, u32[]{:S(2)}) collective-permute-start(bf16[352,2048]{1,0:T(8,128)(2,1)} %get-tuple-element.251), channel_id=1, source_target_pairs={{0,8},{24,16},{1,9},{25,17},{2,10},{26,18},{3,11},{27,19},{4,12},{... | collective-permute-start | bytes 4325384 | tf_op jit(solution)/shard_map/ppermute | solution.py:303
  298.7 36.4 %collective-permute-start.37 = (bf16[384,2048]{1,0:T(8,128)(2,1)}, bf16[384,2048]{1,0:T(8,128)(2,1)}, u32[]{:S(2)}, u32[]{:S(2)}) collective-permute-start(bf16[384,2048]{1,0:T(8,128)(2,1)} %add_convert_fusion.4), channel_id=1, source_target_pairs={{8,0},{16,24},{9,1},{17,25},{10,2},{18,26},{11,3},{19,27},{12,4},{... | collective-permute-start | bytes 4718600 | tf_op jit(solution)/shard_map/ppermute | solution.py:307
  338.5 43.0 %collective-permute-start.42 = (bf16[320,2048]{1,0:T(8,128)(2,1)}, bf16[320,2048]{1,0:T(8,128)(2,1)}, u32[]{:S(2)}, u32[]{:S(2)}) collective-permute-start(bf16[320,2048]{1,0:T(8,128)(2,1)} %add_convert_fusion.14), channel_id=1, source_target_pairs={{8,0},{16,24},{9,1},{17,25},{10,2},{18,26},{11,3},{19,27},{12,4},{... | collective-permute-start | bytes 3932168 | tf_op jit(solution)/shard_map/ppermute | solution.py:307
  342.3 39.2 %collective-permute-start.41 = (bf16[352,2048]{1,0:T(8,128)(2,1)S(1)}, bf16[352,2048]{1,0:T(8,128)(2,1)}, u32[]{:S(2)}, u32[]{:S(2)}) collective-permute-start(bf16[352,2048]{1,0:T(8,128)(2,1)S(1)} %add_convert_fusion.13), channel_id=1, source_target_pairs={{8,16},{16,8},{9,17},{17,9},{10,18},{18,10},{11,19},{19,11},{12,20... | collective-permute-start | bytes 4325384 | tf_op jit(solution)/shard_map/ppermute | solution.py:305
  344.1 37.7 %collective-permute-start.40 = (bf16[352,2048]{1,0:T(8,128)(2,1)S(1)}, bf16[352,2048]{1,0:T(8,128)(2,1)}, u32[]{:S(2)}, u32[]{:S(2)}) collective-permute-start(bf16[352,2048]{1,0:T(8,128)(2,1)S(1)} %copy-done.39), channel_id=1, source_target_pairs={{0,8},{24,16},{1,9},{25,17},{2,10},{26,18},{3,11},{27,19},{4,12},{... | collective-permute-start | bytes 4325384 | tf_op jit(solution)/shard_map/ppermute | solution.py:303
  390.1 54.4 %collective-permute-start.47 = (bf16[352,2048]{1,0:T(8,128)(2,1)S(1)}, bf16[352,2048]{1,0:T(8,128)(2,1)}, u32[]{:S(2)}, u32[]{:S(2)}) collective-permute-start(bf16[352,2048]{1,0:T(8,128)(2,1)S(1)} %add_convert_fusion.11), channel_id=1, source_target_pairs={{8,0},{16,24},{9,1},{17,25},{10,2},{18,26},{11,3},{19,27},{12,4},{... | collective-permute-start | bytes 4325384 | tf_op jit(solution)/shard_map/ppermute | solution.py:307
  393.3 51.2 %collective-permute-start.46 = (bf16[352,2048]{1,0:T(8,128)(2,1)S(1)}, bf16[352,2048]{1,0:T(8,128)(2,1)}, u32[]{:S(2)}, u32[]{:S(2)}) collective-permute-start(bf16[352,2048]{1,0:T(8,128)(2,1)S(1)} %add_convert_fusion.12), channel_id=1, source_target_pairs={{8,16},{16,8},{9,17},{17,9},{10,18},{18,10},{11,19},{19,11},{12,20... | collective-permute-start | bytes 4325384 | tf_op jit(solution)/shard_map/ppermute | solution.py:305
  395.1 49.3 %collective-permute-start.45 = (bf16[352,2048]{1,0:T(8,128)(2,1)}, bf16[352,2048]{1,0:T(8,128)(2,1)}, u32[]{:S(2)}, u32[]{:S(2)}) collective-permute-start(bf16[352,2048]{1,0:T(8,128)(2,1)} %get-tuple-element.278), channel_id=1, source_target_pairs={{0,8},{24,16},{1,9},{25,17},{2,10},{26,18},{3,11},{27,19},{4,12},{... | collective-permute-start | bytes 4325384 | tf_op jit(solution)/shard_map/ppermute | solution.py:303
  447.1 44.0 %collective-permute-start.53 = (bf16[352,2048]{1,0:T(8,128)(2,1)S(1)}, bf16[352,2048]{1,0:T(8,128)(2,1)S(1)}, u32[]{:S(2)}, u32[]{:S(2)}) collective-permute-start(bf16[352,2048]{1,0:T(8,128)(2,1)S(1)} %add_convert_fusion.9), channel_id=1, source_target_pairs={{8,0},{16,24},{9,1},{17,25},{10,2},{18,26},{11,3},{19,27},{12,4},{... | collective-permute-start | bytes 4325384 | tf_op jit(solution)/shard_map/ppermute | solution.py:307
  451.9 39.2 %collective-permute-start.52 = (bf16[352,2048]{1,0:T(8,128)(2,1)S(1)}, bf16[352,2048]{1,0:T(8,128)(2,1)S(1)}, u32[]{:S(2)}, u32[]{:S(2)}) collective-permute-start(bf16[352,2048]{1,0:T(8,128)(2,1)S(1)} %add_convert_fusion.10), channel_id=1, source_target_pairs={{8,16},{16,8},{9,17},{17,9},{10,18},{18,10},{11,19},{19,11},{12,20... | collective-permute-start | bytes 4325384 | tf_op jit(solution)/shard_map/ppermute | solution.py:305
  452.7 38.4 %collective-permute-start.51 = (bf16[352,2048]{1,0:T(8,128)(2,1)S(1)}, bf16[352,2048]{1,0:T(8,128)(2,1)S(1)}, u32[]{:S(2)}, u32[]{:S(2)}) collective-permute-start(bf16[352,2048]{1,0:T(8,128)(2,1)S(1)} %get-tuple-element.308), channel_id=1, source_target_pairs={{0,8},{24,16},{1,9},{25,17},{2,10},{26,18},{3,11},{27,19},{4,12},{... | collective-permute-start | bytes 4325384 | tf_op jit(solution)/shard_map/ppermute | solution.py:303
  504.9 46.5 %collective-permute-start.63 = (bf16[256,2048]{1,0:T(8,128)(2,1)S(1)}, bf16[256,2048]{1,0:T(8,128)(2,1)S(1)}, u32[]{:S(2)}, u32[]{:S(2)}) collective-permute-start(bf16[256,2048]{1,0:T(8,128)(2,1)S(1)} %copy-done.41), channel_id=1, source_target_pairs={{0,8},{24,16},{1,9},{25,17},{2,10},{26,18},{3,11},{27,19},{4,12},{... | collective-permute-start | bytes 3145736 | tf_op jit(solution)/shard_map/ppermute | solution.py:303
  513.3 38.1 %collective-permute-start.65 = (bf16[352,2048]{1,0:T(8,128)(2,1)S(1)}, bf16[352,2048]{1,0:T(8,128)(2,1)S(1)}, u32[]{:S(2)}, u32[]{:S(2)}) collective-permute-start(bf16[352,2048]{1,0:T(8,128)(2,1)S(1)} %add_convert_fusion.7), channel_id=1, source_target_pairs={{8,0},{16,24},{9,1},{17,25},{10,2},{18,26},{11,3},{19,27},{12,4},{... | collective-permute-start | bytes 4325384 | tf_op jit(solution)/shard_map/ppermute | solution.py:307
  552.0 36.2 %collective-permute-start.75 = (bf16[352,2048]{1,0:T(8,128)(2,1)S(1)}, bf16[352,2048]{1,0:T(8,128)(2,1)S(1)}, u32[]{:S(2)}, u32[]{:S(2)}) collective-permute-start(bf16[352,2048]{1,0:T(8,128)(2,1)S(1)} %add_convert_fusion.6), channel_id=1, source_target_pairs={{8,0},{16,24},{9,1},{17,25},{10,2},{18,26},{11,3},{19,27},{12,4},{... | collective-permute-start | bytes 4325384 | tf_op jit(solution)/shard_map/ppermute | solution.py:307
  553.8 32.7 %collective-permute-start.74 = (bf16[256,2048]{1,0:T(8,128)(2,1)S(1)}, bf16[256,2048]{1,0:T(8,128)(2,1)S(1)}, u32[]{:S(2)}, u32[]{:S(2)}) collective-permute-start(bf16[256,2048]{1,0:T(8,128)(2,1)S(1)} %add_convert_fusion.19), channel_id=1, source_target_pairs={{8,16},{16,8},{9,17},{17,9},{10,18},{18,10},{11,19},{19,11},{12,20... | collective-permute-start | bytes 3145736 | tf_op jit(solution)/shard_map/ppermute | solution.py:305
  613.8 33.3 %collective-permute-start.79 = (bf16[2048,256]{1,0:T(8,128)(2,1)S(1)}, bf16[2048,256]{1,0:T(8,128)(2,1)S(1)}, u32[]{:S(2)}, u32[]{:S(2)}) collective-permute-start(bf16[2048,256]{1,0:T(8,128)(2,1)S(1)} %add_convert_fusion.16), channel_id=1, source_target_pairs={{8,0},{16,24},{9,1},{17,25},{10,2},{18,26},{11,3},{19,27},{12,4},{... | collective-permute-start | bytes 3145736 | tf_op jit(solution)/shard_map/ppermute | solution.py:307
  (166 other events, 2444.8 us)
Sparse Core Ops, SparseCore 0:
  25.2 28.2 all-gather.1

commit v2 on v1

--- a/solution.py
+++ b/solution.py
@@ -9,6 +9,10 @@
 
 HEAD = 128
 KEY_BLOCK = 256
+JOIN_COST = 8_000_000_000
+MERGE = True
+BACK_COST = 1
+FORTH_COST = 60
 SMALL_SHIFT = 1e-05
 ROPE_BASE = 10000.0
 NEG_FILL = -1e30
@@ -171,7 +175,7 @@
         ),
         out_shape=[jax.ShapeDtypeStruct(s, t) for s, t in zip(shapes, (BF16, BF16, F32))],
         compiler_params=pltpu.CompilerParams(vmem_limit_bytes=48 * 1024 * 1024),
-        cost_estimate=pl.CostEstimate(flops=flat * wide * span, bytes_accessed=kv.size, transcendentals=0),
+        cost_estimate=pl.CostEstimate(flops=FORTH_COST * flat * wide * span, bytes_accessed=kv.size, transcendentals=0),
         name="attention_forward",
     )(place, lengths, *parts, query_weights, kv, cosine, sine)
 
@@ -254,9 +258,27 @@
             jax.ShapeDtypeStruct(kv.shape, F32),
         ],
         compiler_params=pltpu.CompilerParams(vmem_limit_bytes=56 * 1024 * 1024),
-        cost_estimate=pl.CostEstimate(flops=flat * wide * span, bytes_accessed=kv.size, transcendentals=0),
+        cost_estimate=pl.CostEstimate(flops=BACK_COST * flat * wide * span, bytes_accessed=kv.size, transcendentals=0),
         name="attention_backward",
     )(place, lengths, *operands)
+
+
+def join_columns(parts):
+    rows, wide = parts[0].shape
+
+    def kernel(*refs):
+        for k in range(len(parts)):
+            refs[-1][:, k * wide : (k + 1) * wide] = refs[k][...]
+
+    return pl.pallas_call(
+        kernel,
+        grid=(4,),
+        in_specs=[pl.BlockSpec((rows // 4, wide), lambda i: (i, 0)) for _ in parts],
+        out_specs=pl.BlockSpec((rows // 4, wide * len(parts)), lambda i: (i, 0)),
+        out_shape=jax.ShapeDtypeStruct((rows, wide * len(parts)), parts[0].dtype),
+        cost_estimate=pl.CostEstimate(flops=JOIN_COST, bytes_accessed=0, transcendentals=0),
+        name="join_columns",
+    )(*parts)
 
 
 def middle_bits(n):
@@ -300,11 +322,19 @@
         arrays, inward, across, outward, others = tie(
             list(arrays), self.inward, self.across, self.outward, others
         )
-        self.inward = [(a, lax.ppermute(a, "dp", [(0, 1), (3, 2)])) for a in arrays]
         pairs = [add_up(own, sent).astype(BF16) for own, sent in inward]
+        totals = [add_up(own, sent).astype(BF16) for own, sent in across]
+        self.inward, self.outward = [], []
+        if MERGE and [a.shape for a in arrays] == [t.shape for t in totals]:
+            for own, total in zip(arrays, totals):
+                sent = jnp.where(self.outer, own, total)
+                sent = lax.ppermute(sent, "dp", [(0, 1), (1, 0), (2, 3), (3, 2)])
+                self.inward.append((own, sent))
+                self.outward.append((total, sent))
+        else:
+            self.inward = [(a, lax.ppermute(a, "dp", [(0, 1), (3, 2)])) for a in arrays]
+            self.outward = [(a, lax.ppermute(a, "dp", [(1, 0), (2, 3)])) for a in totals]
         self.across = [(a, lax.ppermute(a, "dp", [(1, 2), (2, 1)])) for a in pairs]
-        totals = [add_up(own, sent).astype(BF16) for own, sent in across]
-        self.outward = [(a, lax.ppermute(a, "dp", [(1, 0), (2, 3)])) for a in totals]
         self.sums += [jnp.where(self.outer, sent, own) for own, sent in outward]
         return others
 
@@ -358,28 +388,29 @@
     return value[:rows], value[rows:]
 
 
-def reduce_begin(count, terms):
+def reduce_begin(count, terms, between):
     n = lax.axis_size("tensor")
     if n != 8:
         parts = []
         for i in range(count):
-            own, other = halves(terms(i, None))
+            own, other = terms(i, None)
             parts.append(add_up(own, swap(other, 1)))
         while len(parts) > 1:
             half = len(parts) // 2
             parts = [add_up(parts[i], swap(parts[half + i].astype(BF16), 2 * half)) for i in range(half)]
+        between(parts[0])
         return parts[0], ()
-    own_d, other_d = halves(terms(3, None))
+    own_d, other_d = (terms(3, None))
     core_d = swap(other_d, 1)
-    own_y, other_y = halves(terms(2, own_d))
+    own_y, other_y = (terms(2, own_d))
     core_y = swap(other_y, 1)
     diagonal = add_up(own_d, core_d).astype(BF16)
     diagonal, own_y = tie(diagonal, own_y)
     first, second = halves(diagonal)
     from_x, from_y = swap(first, 2), swap(second, 4)
-    own_x, other_x = halves(terms(1, diagonal))
+    own_x, other_x = (terms(1, between(diagonal)))
     core_x = swap(other_x, 1)
-    own, other = halves(terms(0, own_x))
+    own, other = (terms(0, own_x))
     core = swap(other, 1)
     low, high = halves(add_up(own_y, core_y))
     for_y = jnp.concatenate([add_up(low, from_x), high]).astype(BF16)
@@ -426,15 +457,16 @@
     far_in = swap(norm_in, top)
     far_in = (far_in, swap(far_in, 1))
     near_in = (norm_in, swap(norm_in, 1))
-    query_weights = jnp.concatenate(gather_middle(query_weight), axis=1)
-    output_weight, query_weights = tie(output_weight, query_weights)
-    output_parts = gather_middle(output_weight)
+    query_weights = join_columns(gather_middle(query_weight))
     heads_width = query_weights.shape[1]
     own_cos, own_sin = rope_block(me * rows, rows)
     kv_raw = dot(norm_in, kv_weight, ((1,), (0,))).reshape(seqs, rows, 2 * HEAD)
     key_raw = kv_raw[..., :HEAD]
     key_own = key_raw * own_cos + jnp.roll(key_raw, HEAD // 2, axis=-1) * own_sin
     kv_own = jnp.concatenate([key_own, kv_raw[..., HEAD:]], axis=-1).astype(BF16)
+
+    output_weight, kv_own = tie(output_weight, kv_own)
+    output_parts = gather_middle(output_weight)
     kv = lax.all_gather(kv_own, "tensor", axis=1, tiled=True)
 
     def place_of(offset):
@@ -462,80 +494,93 @@
     for_far = add_up(far_portions[0], swap(far_portions[1], 1)).astype(BF16)
     for_far, near_mixed = tie(for_far, near_result[0])
     from_far = swap(for_far, top)
+    def slopes_of(blocks):
+        return [dot(block, down_weight, ((1,), (1,))) for block in blocks]
+
+    def with_core(part):
+        return part, swap(part, 1)
+
     near_portions = portions_of(near_mixed)
     near_core = swap(near_portions[1], 1)
     if n == 8:
         grad_out, _ = tie(grad_out, far_mixed)
-        grad_parts = [grad_out, swap(grad_out, 2), grad_far, swap(grad_far, 2)]
-        from_far, grad_parts = tie(from_far, grad_parts)
-        grad_pairs = [(part, swap(part, 1)) for part in grad_parts]
-    else:
-        grad_pairs = gather_pairs(grad_out)
-    grad_chunks = [jnp.concatenate(c) for c in grad_pairs]
+        grad_side = swap(grad_out, 2)
+        size = flat // 2
+        own_slopes = slopes_of([*with_core(grad_out), *with_core(grad_far)])
+        from_far, grad_side, grad_far, own_slopes = tie(from_far, grad_side, grad_far, own_slopes)
+        grad_diagonal = [swap(grad_side[:size], 4), swap(grad_far[size:], 2)]
     attn_out = add_up(near_portions[0], near_core, from_far)
     hidden = x + valid * attn_out.reshape(seqs, rows, width)
 
     chips = n // 2
     norm_mid = normed(hidden, mlp_gain).astype(BF16).reshape(flat, width)
     gate_rows, up_rows = gate_weight.T, up_weight.T
-    mid_chunks, acts, g_gates, g_ups = [], [], [], []
-
-    def slope_of(i):
-        return dot(grad_chunks[i], down_weight, ((1,), (1,)))
-
-    def forward_chunk(pair, slope):
-        mid = jnp.concatenate(pair)
-        gate = dot(mid, gate_rows, ((1,), (1,)))
-        up = dot(mid, up_rows, ((1,), (1,)))
-        sig = 1.0 / (1.0 + jnp.exp(-gate))
-        silu = gate * sig
-        mid_chunks.append(mid)
-        acts.append((silu * up).astype(BF16))
-        g_gates.append((slope * up * sig * (1.0 + gate * (1.0 - sig))).astype(BF16))
-        g_ups.append((slope * silu).astype(BF16))
+
+    mids, acts, g_gates, g_ups = [], [], [], []
+
+    def forward_blocks(blocks, slopes):
+        for mid, slope in zip(blocks, slopes):
+            gate = dot(mid, gate_rows, ((1,), (1,)))
+            up = dot(mid, up_rows, ((1,), (1,)))
+            sig = 1.0 / (1.0 + jnp.exp(-gate))
+            silu = gate * sig
+            mids.append(mid)
+            acts.append((silu * up).astype(BF16))
+            g_gates.append((slope * up * sig * (1.0 + gate * (1.0 - sig))).astype(BF16))
+            g_ups.append((slope * silu).astype(BF16))
+
+    def diagonal_blocks(parts):
+        return [jnp.concatenate(p) for p in zip(*[with_core(part) for part in parts])]
 
     if n == 8:
         at_x, at_y = gather_near(norm_mid)
-        forward_chunk((norm_mid, swap(norm_mid, 1)), slope_of(0))
-        slopes = [slope_of(i) for i in range(1, 4)]
-        at_x, at_y, slopes, acts[0] = tie(at_x, at_y, slopes, acts[0])
-        size = flat // 2
+        grads = [*with_core(grad_out), *with_core(grad_side)]
+        slopes = own_slopes[:2] + slopes_of(grads[2:]) + own_slopes[2:]
+        forward_blocks(with_core(norm_mid), slopes[:2])
+        at_x, at_y, slopes, acts[1] = tie(at_x, at_y, slopes, acts[1])
         diagonal = [swap(at_x[:size], 4), swap(at_y[size:], 2)]
-        for i, part in enumerate((at_x, at_y)):
-            forward_chunk((part, swap(part, 1)), slopes[i])
-        diagonal, acts[1], acts[2] = tie(diagonal, acts[1], acts[2])
-        forward_chunk((*diagonal, *[swap(part, 1) for part in diagonal]), slopes[2])
+        grad_diagonal, _ = tie(grad_diagonal, at_x)
+        grads += [*with_core(grad_far), *diagonal_blocks(grad_diagonal)]
+        forward_blocks((*with_core(at_x), *with_core(at_y)), slopes[2:6])
+        grad_down = dot(jnp.concatenate(acts), jnp.concatenate(grads[:6]), ((0,), (0,)))
+        diagonal, grad_down = tie(diagonal, grad_down)
+        forward_blocks(diagonal_blocks(diagonal), slopes_of(grads[6:]))
     else:
-        for i, pair in enumerate(gather_pairs(norm_mid)):
-            forward_chunk(pair, slope_of(i))
+        grads = [block for pair in gather_pairs(grad_out) for block in pair]
+        forward_blocks([block for pair in gather_pairs(norm_mid) for block in pair], slopes_of(grads))
+        grad_down = dot(jnp.concatenate(acts[:-2]), jnp.concatenate(grads[:-2]), ((0,), (0,)))
+
+    def mid_term(r):
+        terms = dot(g_gates[r], gate_rows, ((1,), (0,))) + dot(g_ups[r], up_rows, ((1,), (0,)))
+        return terms.astype(BF16)
 
     def mid_terms(i, after):
-        left, right = g_gates[i], g_ups[i]
-        if after is not None:
-            left, right, _ = tie(left, right, after)
-        terms = dot(left, gate_rows, ((1,), (0,))) + dot(right, up_rows, ((1,), (0,)))
-        return terms.astype(BF16)
-
-    sums = LineSum()
-    act_all, grad_all = jnp.concatenate(acts), jnp.concatenate(grad_chunks)
-    cut = (act_all.shape[1] // 2 + 127) // 128 * 128
-    grad_down = dot(act_all[:, :cut], grad_all, ((0,), (0,)), BF16)
-
-    g_gates, g_ups, act_all = sums.advance([grad_down], (g_gates, g_ups, act_all))
-    mid_own, mid_sent = reduce_begin(chips, mid_terms)
-    grad_rest = dot(act_all[:, cut:], grad_all, ((0,), (0,)), BF16)
-
-    mid_sent, g_gates, g_ups = sums.advance([grad_rest], (mid_sent, g_gates, g_ups))
-    mid_all = jnp.concatenate(mid_chunks)
+        for k in (2 * i, 2 * i + 1):
+            if after is not None:
+                g_gates[k], g_ups[k], _ = tie(g_gates[k], g_ups[k], after)
+        return mid_term(2 * i), mid_term(2 * i + 1)
+
+    sums, down_parts = LineSum(), []
+
+    def down_gradient(after):
+        last, after = tie(acts[-2:], after)
+        term = dot(jnp.concatenate(last), jnp.concatenate(grads[-2:]), ((0,), (0,)))
+        down_parts.extend(halves((grad_down + term).astype(BF16)))
+        return sums.advance([down_parts[0]], after)
+
+    mid_own, mid_sent = reduce_begin(chips, mid_terms, down_gradient)
+    grad_mid = reduce_end(mid_own, mid_sent).reshape(seqs, rows, width)
+
+    g_gates, g_ups, mids = sums.advance([down_parts[1]], (g_gates, g_ups, mids))
+    mid_all = jnp.concatenate(mids)
     grad_gate = halves(dot(jnp.concatenate(g_gates), mid_all, ((0,), (0,)), BF16))
-    grad_mid = reduce_end(mid_own, mid_sent).reshape(seqs, rows, width)
     back, mlp_gain_part = norm_back(hidden, mlp_gain, grad_mid)
     grad_hidden = grad_y + back
     grad_attn = (valid * grad_hidden).astype(BF16).reshape(flat, width)
-
-    grad_attn, g_ups = sums.advance([grad_gate[0]], (grad_attn, g_ups))
     far_grad = swap(grad_attn, top)
     near_grad = (grad_attn, swap(grad_attn, 1))
+
+    g_ups = sums.advance([grad_gate[0]], g_ups)
     grad_up = halves(dot(jnp.concatenate(g_ups), mid_all, ((0,), (0,)), BF16))
 
     def attend_back(part, result, place, table):
@@ -550,9 +595,9 @@
     far_grad = (far_grad, swap(far_grad, 1))
     far_q, far_terms, far_kv = attend_back(far_grad, far_result, far_place, far_table)
     for_far = add_up(far_terms[0], swap(far_terms[1], 1)).astype(BF16)
+    from_far = swap(for_far, top)
 
     for_far, near_grad, far_grad = sums.advance([grad_up[0]], (for_far, near_grad, far_grad))
-    from_far = swap(for_far, top)
     unit = output_weight.shape[0]
     mixed = [r[0][i] for r in (near_result, far_result) for i in range(2)]
     wo_full = product(mixed, [*near_grad, *far_grad])
@@ -566,9 +611,9 @@
     )
     kv_blocks = (near_kv + far_kv).astype(BF16).reshape(seqs, n, rows, 2 * HEAD).swapaxes(0, 1)
     kv_sum = reduce_blocks(kv_blocks)
-    wq_full = product([*near_in, *far_in], [near_q[0], near_q[1], far_q[0], far_q[1]])
+    wq_full = product([near_q[0], near_q[1], far_q[0], far_q[1]], [*near_in, *far_in])
     wq_full, kv_sum = tie(wq_full, kv_sum)
-    wq_part = reduce_middle([wq_full[:, i * unit : (i + 1) * unit] for i in range(heads_width // unit)])
+    wq_part = reduce_middle([wq_full[i * unit : (i + 1) * unit] for i in range(heads_width // unit)])
     wq_part = wq_part.astype(BF16)
     key_grad = kv_sum[..., :HEAD]
     key_grad = key_grad * own_cos - jnp.roll(key_grad, HEAD // 2, axis=-1) * own_sin
@@ -579,22 +624,21 @@
     back, attn_gain_part = norm_back(x, attn_gain, grad_in.reshape(seqs, rows, width))
     grad_tokens = grad_hidden + back
 
-    kv_portion, attn_gain_part, wq_part, acts = sums.advance(
-        [wo_part], (kv_portion, attn_gain_part, wq_part, acts)
-    )
+    kv_portion, attn_gain_part = sums.advance([wo_part], (kv_portion, attn_gain_part))
     gains = jnp.concatenate([attn_gain_part, mlp_gain_part]).reshape(-1, 2 * HEAD)
     shared = jnp.concatenate([kv_portion + pair_grad[0, 0], gains])
     shared = jnp.pad(shared, ((0, -shared.shape[0] % (16 * n)), (0, 0))).astype(BF16)
     shared = reduce_blocks(shared.reshape(n, -1, 2 * HEAD)).astype(BF16)
 
+
+    acts = sums.advance([wq_part, shared], acts)
+
     def out_terms(i, after):
-        left = acts[i] if after is None else tie(acts[i], after)[0]
-        return dot(left, down_weight, ((1,), (0,)), BF16)
-
-    acts, shared = tie(acts, shared)
-    out_own, out_sent = reduce_begin(chips, out_terms)
-
-    out_sent = sums.advance([wq_part, shared], out_sent)
+        left = acts[2 * i : 2 * i + 2]
+        left = left if after is None else tie(left, after)[0]
+        return [dot(part, down_weight, ((1,), (0,)), BF16) for part in left]
+
+    out_own, out_sent = reduce_begin(chips, out_terms, lambda after: after)
     rows_out = reduce_end(out_own, out_sent)
     output = (hidden + valid * rows_out.reshape(seqs, rows, width)).astype(BF16)
     sums.advance([])
@@ -606,7 +650,7 @@
     return (
         output,
         grad_tokens,
-        wq_sum.astype(F32),
+        wq_sum.astype(F32).T,
         shared[:width, :HEAD],
         shared[:width, HEAD:],
         wo_sum.astype(F32),

time: 681 us -> 645 us (0.947)
  waiting for transfers between devices: 267 us -> 239 us
  starting transfers between devices: 113 us -> 101 us
  local copies, waits for them, and re-layouts: 54.2 us -> 42.7 us
  other arithmetic: 81.5 us -> 88.5 us
    ppermute x57 -> x60, waiting for transfers between devices: 199 us -> 89.6 us  [swap(): return lax.ppermute(values, 'tensor', [(i, i ^ bit) for i in range(n)])]
    ppermute x0 -> x4, waiting for transfers between devices: none -> 60.1 us  [advance(): sent = lax.ppermute(sent, 'dp', [(0, 1), (1, 0), (2, 3), (3, 2)])]
    ppermute x9 -> x5, waiting for transfers between devices: 20.4 us -> 50.1 us  [advance(): self.inward = [(a, lax.ppermute(a, 'dp', [(0, 1), (3, 2)])) for a in arrays]]
    ppermute x9 -> x5, starting transfers between devices: 52.6 us -> 27.1 us  [advance(): self.inward = [(a, lax.ppermute(a, 'dp', [(0, 1), (3, 2)])) for a in arrays]]
    ppermute x0 -> x4, starting transfers between devices: none -> 15.5 us  [advance(): sent = lax.ppermute(sent, 'dp', [(0, 1), (1, 0), (2, 3), (3, 2)])]
    select_n x0 -> x4, other arithmetic: none -> 11.4 us  [advance(): sent = jnp.where(self.outer, own, total)]
    unnamed x229 -> x307, local copies, waits for them, and re-layouts: 33.6 us -> 22.5 us
    ppermute x9 -> x5, waiting for transfers between devices: 47.7 us -> 39.2 us  [advance(): lax.ppermute(a, 'dp', [(1, 0), (2, 3)])]
  transfers between devices with their start and end apart: 85 -> 84, of which waited for: 30 -> 27; matrix products, arithmetic and copies ran while one was open for 27% -> 29% of each run, Pallas kernels for 7% -> 8%
where the time goes in v2:
time: 645 us; the launch traced here: 635 us
  waiting for transfers between devices  239 us (37%)
  starting transfers between devices  101 us (16%)
  matrix products  98.1 us (15%)
  other arithmetic  88.5 us (14%)
  Pallas kernels  48.7 us (8%)
  local copies, waits for them, and re-layouts  42.7 us (7%)
  between operations  17.6 us (3%)
    dot_general x61, matrix products, dot(): lax.dot_general(a, b, (dims, ((), ())), preferred_element_type=F32)  98.1 us
    ppermute x60, waiting for transfers between devices, swap(): return lax.ppermute(values, 'tensor', [(i, i ^ bit) for i in range(n)])  89.6 us
    ppermute x4, waiting for transfers between devices, advance(): sent = lax.ppermute(sent, 'dp', [(0, 1), (1, 0), (2, 3), (3, 2)])  60.1 us
    ppermute x5, waiting for transfers between devices, advance(): self.inward = [(a, lax.ppermute(a, 'dp', [(0, 1), (3, 2)])) for a in arrays]  50.1 us
    ppermute x60, starting transfers between devices, swap(): return lax.ppermute(values, 'tensor', [(i, i ^ bit) for i in range(n)])  40.4 us
    ppermute x5, waiting for transfers between devices, advance(): lax.ppermute(a, 'dp', [(1, 0), (2, 3)])  39.2 us
    pallas_call x2, Pallas kernels, attention_backward(): pl.pallas_call(backward_kernel, grid_spec=pltpu.PrefetchScalarGridSpec(nu...  28.3 us
    ppermute x5, starting transfers between devices, advance(): self.inward = [(a, lax.ppermute(a, 'dp', [(0, 1), (3, 2)])) for a in arrays]  27.1 us
  transfers between devices with their start and end apart: 84, of which 27 were waited for; matrix products, arithmetic and copies ran while one was open for 29% of the time, Pallas kernels for 8%

profile of v2, /device:TPU:0, one launch (start us, length us, event | category | flops | bytes accessed | tf_op | source)
XLA Modules:
  0.0 635.3 jit_solution(13239463380951595147)
XLA Ops:
  33.9 7.5 %collective-permute-done.1.x0_ref = bf16[256,2048]{1,0:T(8,128)(2,1)} collective-permute-done((bf16[256,2048]{1,0:T(8,128)(2,1)}, bf16[256,2048]{1,0:T(8,128)(2,1)}, u32[]{:S(2)}, u32[]{:S(2)}) %collective-permute-start.1) | collective-permute-done | bytes 1048608 | tf_op jit(solution)/shard_map/ppermute | solution.py:51
  41.4 13.8 %collective-permute-done.4.refs_1_ = bf16[2048,256]{1,0:T(8,128)(2,1)} collective-permute-done((bf16[2048,256]{1,0:T(8,128)(2,1)}, bf16[2048,256]{1,0:T(8,128)(2,1)}, u32[]{:S(2)}, u32[]{:S(2)}) %collective-permute-start.4) | collective-permute-done | bytes 1048608 | tf_op jit(solution)/shard_map/ppermute | solution.py:51
  60.2 7.1 %attention_forward.2 = (bf16[2,256,512]{2,1,0:T(8,128)(2,1)S(1)}, bf16[2,2,512,128]{3,2,1,0:T(8,128)(2,1)S(1)}, f32[2,2,8,512]{3,2,1,0:T(8,128)S(1)}) custom-call(s32[2]{0:T(128)S(1)} %pad_add_fusion.1.place, s32[2]{0:T(128)S(1)} %copy-done.12, bf16[256,2048]{1,0:T(8,128)(2,1)} %bitcast.3.x0_ref, bf16[256,2048]{1,0:T(8,128)(2,1)} %collective-permute-done.3.x1_ref, ...), custom_call_target="tpu_custom_call" | custom-call | flops 8053063680 | bytes 524288 | tf_op jit(solution)/shard_map/attention_forward/pallas_call | solution.py:160
  68.8 9.5 %attention_forward.3 = (bf16[2,256,512]{2,1,0:T(8,128)(2,1)S(1)}, bf16[2,2,512,128]{3,2,1,0:T(8,128)(2,1)S(1)}, f32[2,2,8,512]{3,2,1,0:T(8,128)S(1)}) custom-call(s32[2]{0:T(128)S(1)} %pad_add_fusion.place, s32[2]{0:T(128)S(1)} %copy-done.12, bf16[256,2048]{1,0:T(8,128)(2,1)} %collective-permute-done.1.x0_ref, ...), custom_call_target="tpu_custom_call" | custom-call | flops 8053063680 | bytes 524288 | tf_op jit(solution)/shard_map/attention_forward/pallas_call | solution.py:160
  95.1 12.8 %collective-permute-done.9 = bf16[256,2048]{1,0:T(8,128)(2,1)S(1)} collective-permute-done((bf16[256,2048]{1,0:T(8,128)(2,1)}, bf16[256,2048]{1,0:T(8,128)(2,1)S(1)}, u32[]{:S(2)}, u32[]{:S(2)}) %collective-permute-start.9) | collective-permute-done | bytes 1048608 | tf_op jit(solution)/shard_map/ppermute | solution.py:51
  107.8 9.4 %collective-permute-done.8 = bf16[256,2048]{1,0:T(8,128)(2,1)S(1)} collective-permute-done((bf16[256,2048]{1,0:T(8,128)(2,1)S(1)}, bf16[256,2048]{1,0:T(8,128)(2,1)S(1)}, u32[]{:S(2)}, u32[]{:S(2)}) %collective-permute-start.8) | collective-permute-done | bytes 1048608 | tf_op jit(solution)/shard_map/ppermute | solution.py:51
  134.0 11.1 %collective-permute-done.12 = bf16[256,2048]{1,0:T(8,128)(2,1)S(1)} collective-permute-done((bf16[256,2048]{1,0:T(8,128)(2,1)S(1)}, bf16[256,2048]{1,0:T(8,128)(2,1)S(1)}, u32[]{:S(2)}, u32[]{:S(2)}) %collective-permute-start.12) | collective-permute-done | bytes 1048608 | tf_op jit(solution)/shard_map/ppermute | solution.py:51
  146.3 9.8 %collective-permute-done.23 = bf16[128,2048]{1,0:T(8,128)(2,1)S(1)} collective-permute-done((bf16[128,2048]{1,0:T(8,128)(2,1)S(1)}, bf16[128,2048]{1,0:T(8,128)(2,1)S(1)}, u32[]{:S(2)}, u32[]{:S(2)}) %collective-permute-start.23) | collective-permute-done | bytes 524320 | tf_op jit(solution)/shard_map/ppermute | solution.py:51
  224.6 17.8 %collective-permute-done.28 = bf16[352,2048]{1,0:T(8,128)(2,1)S(1)} collective-permute-done((bf16[352,2048]{1,0:T(8,128)(2,1)S(1)}, bf16[352,2048]{1,0:T(8,128)(2,1)S(1)}, u32[]{:S(2)}, u32[]{:S(2)}) %collective-permute-start.28) | collective-permute-done | bytes 1441824 | tf_op jit(solution)/shard_map/ppermute | solution.py:335
  246.0 7.6 %collective-permute-start.29 = (bf16[352,2048]{1,0:T(8,128)(2,1)}, bf16[352,2048]{1,0:T(8,128)(2,1)}, u32[]{:S(2)}, u32[]{:S(2)}) collective-permute-start(bf16[352,2048]{1,0:T(8,128)(2,1)} %get-tuple-element.289), channel_id=1, source_target_pairs={{0,8},{24,16},{1,9},{25,17},{2,10},{26,18},{3,11},{27,19},{4,12},{... | collective-permute-start | bytes 4325384 | tf_op jit(solution)/shard_map/ppermute | solution.py:335
  258.4 6.4 %convolution_convert_fusion.1 = bf16[704,2048]{1,0:T(8,128)(2,1)S(1)} fusion(bf16[2048,704]{0,1:T(8,128)(2,1)S(1)} %constant_dynamic-update-slice_fusion.20, bf16[2048,2048]{1,0:T(8,128)(2,1)S(1)} %constant_dynamic-update-slice_fusion.28), kind=kOutput, calls=%fused_computation.26 | convolution fusion | flops 5907021824 | bytes 14155776 | tf_op jit(solution)/shard_map/dot_general | solution.py:55
  271.9 10.8 %collective-permute-done.29 = bf16[352,2048]{1,0:T(8,128)(2,1)} collective-permute-done((bf16[352,2048]{1,0:T(8,128)(2,1)}, bf16[352,2048]{1,0:T(8,128)(2,1)}, u32[]{:S(2)}, u32[]{:S(2)}) %collective-permute-start.29) | collective-permute-done | bytes 1441824 | tf_op jit(solution)/shard_map/ppermute | solution.py:335
  295.3 10.8 %convolution_convert_fusion = bf16[704,2048]{1,0:T(8,128)(2,1)} fusion(bf16[2048,704]{0,1:T(8,128)(2,1)S(1)} %constant_dynamic-update-slice_fusion.36, bf16[2048,2048]{1,0:T(8,128)(2,1)} %copy-done.123), kind=kOutput, calls=%fused_computation.25 | convolution fusion | flops 5907021824 | bytes 14155776 | tf_op jit(solution)/shard_map/dot_general | solution.py:55
  306.1 18.0 %collective-permute-done.31 = bf16[352,2048]{1,0:T(8,128)(2,1)S(1)} collective-permute-done((bf16[352,2048]{1,0:T(8,128)(2,1)S(1)}, bf16[352,2048]{1,0:T(8,128)(2,1)S(1)}, u32[]{:S(2)}, u32[]{:S(2)}) %collective-permute-start.31) | collective-permute-done | bytes 1441824 | tf_op jit(solution)/shard_map/ppermute | solution.py:331
  334.9 15.4 %attention_backward.2 = (bf16[2,256,512]{2,1,0:T(8,128)(2,1)}, bf16[2,256,2048]{2,1,0:T(8,128)(2,1)}, f32[2,1024,256]{2,1,0:T(8,128)}) custom-call(s32[2]{0:T(128)} %copy-done.14, s32[2]{0:T(128)} %lengths.7, bf16[256,2048]{1,0:T(8,128)(2,1)} %collective-permute-done.40.g0_ref, bf16[256,2048]{1,0:T(8,128)(2,1)} %copy-done.87, bf16[512,2048]{1,0:T(8,128)(2,1)} %copy-done.16, ...), custom_call_target="tpu_custom_call" | custom-call | flops 134217728 | bytes 524288 | tf_op jit(solution)/shard_map/attention_backward/pallas_call | solution.py:246
  357.9 8.2 %collective-permute-done.42 = bf16[352,2048]{1,0:T(8,128)(2,1)} collective-permute-done((bf16[352,2048]{1,0:T(8,128)(2,1)}, bf16[352,2048]{1,0:T(8,128)(2,1)}, u32[]{:S(2)}, u32[]{:S(2)}) %collective-permute-start.42) | collective-permute-done | bytes 1441824 | tf_op jit(solution)/shard_map/ppermute | solution.py:331
  374.3 12.9 %attention_backward.3 = (bf16[2,256,512]{2,1,0:T(8,128)(2,1)}, bf16[2,256,2048]{2,1,0:T(8,128)(2,1)}, f32[2,1024,256]{2,1,0:T(8,128)}) custom-call(s32[2]{0:T(128)} %copy-done.13, s32[2]{0:T(128)} %lengths.7, bf16[256,2048]{1,0:T(8,128)(2,1)} %bitcast.22.g0_ref, bf16[256,2048]{1,0:T(8,128)(2,1)} %collective-permute-done.41.g1_ref, ...), custom_call_target="tpu_custom_call" | custom-call | flops 134217728 | bytes 524288 | tf_op jit(solution)/shard_map/attention_backward/pallas_call | solution.py:246
  405.0 24.4 %collective-permute-done.46 = bf16[352,2048]{1,0:T(8,128)(2,1)S(1)} collective-permute-done((bf16[352,2048]{1,0:T(8,128)(2,1)S(1)}, bf16[352,2048]{1,0:T(8,128)(2,1)S(1)}, u32[]{:S(2)}, u32[]{:S(2)}) %collective-permute-start.46) | collective-permute-done | bytes 1441824 | tf_op jit(solution)/shard_map/ppermute | solution.py:331
  460.5 9.5 %collective-permute-done.55 = bf16[352,2048]{1,0:T(8,128)(2,1)S(1)} collective-permute-done((bf16[352,2048]{1,0:T(8,128)(2,1)S(1)}, bf16[352,2048]{1,0:T(8,128)(2,1)S(1)}, u32[]{:S(2)}, u32[]{:S(2)}) %collective-permute-start.55) | collective-permute-done | bytes 1441824 | tf_op jit(solution)/shard_map/ppermute | solution.py:331
  500.3 8.4 %collective-permute-done.60 = bf16[256,2048]{1,0:T(8,128)(2,1)S(1)} collective-permute-done((bf16[256,2048]{1,0:T(8,128)(2,1)S(1)}, bf16[256,2048]{1,0:T(8,128)(2,1)S(1)}, u32[]{:S(2)}, u32[]{:S(2)}) %collective-permute-start.60) | collective-permute-done | bytes 1048608 | tf_op jit(solution)/shard_map/ppermute | solution.py:335
  513.8 8.5 %collective-permute-start.71 = (bf16[256,2048]{1,0:T(8,128)(2,1)S(1)}, bf16[256,2048]{1,0:T(8,128)(2,1)S(1)}, u32[]{:S(2)}, u32[]{:S(2)}) collective-permute-start(bf16[256,2048]{1,0:T(8,128)(2,1)S(1)} %add_convert_fusion.19), channel_id=1, source_target_pairs={{0,8},{24,16},{1,9},{25,17},{2,10},{26,18},{3,11},{27,19},{4,12},{... | collective-permute-start | bytes 3145736 | tf_op jit(solution)/shard_map/ppermute | solution.py:335
  533.1 13.1 %collective-permute-done.72 = bf16[272,256]{1,0:T(8,128)(2,1)S(1)} collective-permute-done((bf16[272,256]{1,0:T(8,128)(2,1)S(1)}, bf16[272,256]{1,0:T(8,128)(2,1)S(1)}, u32[]{:S(2)}, u32[]{:S(2)}) %collective-permute-start.72) | collective-permute-done | bytes 139296 | tf_op jit(solution)/shard_map/ppermute | solution.py:335
  562.7 10.9 %collective-permute-done.77 = bf16[256,2048]{1,0:T(8,128)(2,1)S(1)} collective-permute-done((bf16[256,2048]{1,0:T(8,128)(2,1)S(1)}, bf16[256,2048]{1,0:T(8,128)(2,1)S(1)}, u32[]{:S(2)}, u32[]{:S(2)}) %collective-permute-start.77) | collective-permute-done | bytes 1048608 | tf_op jit(solution)/shard_map/ppermute | solution.py:336
  579.6 28.3 %collective-permute-done.79 = bf16[272,256]{1,0:T(8,128)(2,1)S(1)} collective-permute-done((bf16[272,256]{1,0:T(8,128)(2,1)S(1)}, bf16[272,256]{1,0:T(8,128)(2,1)S(1)}, u32[]{:S(2)}, u32[]{:S(2)}) %collective-permute-start.79) | collective-permute-done | bytes 139296 | tf_op jit(solution)/shard_map/ppermute | solution.py:336
  (681 shorter events, 325.7 us)
Async XLA Ops:
  7.2 51.8 %all-gather.2.cloned.1.call-start = ((), (), s32[]{:S(2)}) async-start(), calls=%async_computation | async-start | bytes 1179648 | tf_op jit(solution)/shard_map/all_gather | solution.py:470
  12.7 46.2 %collective-permute-start.3 = (bf16[256,2048]{1,0:T(8,128)(2,1)}, bf16[256,2048]{1,0:T(8,128)(2,1)}, u32[]{:S(2)}, u32[]{:S(2)}) collective-permute-start(bf16[256,2048]{1,0:T(8,128)(2,1)} %bitcast.3.x0_ref), channel_id=1, source_target_pairs={{0,1},{1,0},{2,3},{3,2},{4,5},{5,4},{6,7},{7,6},{8,9},{9,8},{10,11... | collective-permute-start | bytes 3145736 | tf_op jit(solution)/shard_map/ppermute | solution.py:51
  26.2 52.2 %collective-permute-start = (bf16[256,2048]{1,0:T(8,128)(2,1)}, bf16[256,2048]{1,0:T(8,128)(2,1)}, u32[]{:S(2)}, u32[]{:S(2)}) collective-permute-start(bf16[256,2048]{1,0:T(8,128)(2,1)} %param.18), channel_id=1, source_target_pairs={{0,2},{1,3},{2,0},{3,1},{4,6},{5,7},{6,4},{7,5},{8,10},{9,11},{10,... | collective-permute-start | bytes 3145736 | tf_op jit(solution)/shard_map/ppermute | solution.py:51
  29.9 48.5 %collective-permute-start.5 = (bf16[256,2048]{1,0:T(8,128)(2,1)}, bf16[256,2048]{1,0:T(8,128)(2,1)}, u32[]{:S(2)}, u32[]{:S(2)}) collective-permute-start(bf16[256,2048]{1,0:T(8,128)(2,1)} %bitcast.14), channel_id=1, source_target_pairs={{0,4},{1,5},{2,6},{3,7},{4,0},{5,1},{6,2},{7,3},{8,12},{9,13},{10,... | collective-permute-start | bytes 3145736 | tf_op jit(solution)/shard_map/ppermute | solution.py:51
  207.7 34.6 %collective-permute-start.28 = (bf16[352,2048]{1,0:T(8,128)(2,1)S(1)}, bf16[352,2048]{1,0:T(8,128)(2,1)S(1)}, u32[]{:S(2)}, u32[]{:S(2)}) collective-permute-start(bf16[352,2048]{1,0:T(8,128)(2,1)S(1)} %get-tuple-element.268), channel_id=1, source_target_pairs={{0,8},{24,16},{1,9},{25,17},{2,10},{26,18},{3,11},{27,19},{4,12},{... | collective-permute-start | bytes 4325384 | tf_op jit(solution)/shard_map/ppermute | solution.py:335
  215.4 51.3 %collective-permute-start.33 = (bf16[256,2048]{1,0:T(8,128)(2,1)S(1)}, bf16[256,2048]{1,0:T(8,128)(2,1)S(1)}, u32[]{:S(2)}, u32[]{:S(2)}) collective-permute-start(bf16[256,2048]{1,0:T(8,128)(2,1)S(1)} %fusion.27), channel_id=1, source_target_pairs={{0,1},{1,0},{2,3},{3,2},{4,5},{5,4},{6,7},{7,6},{8,9},{9,8},{10,11... | collective-permute-start | bytes 3145736 | tf_op jit(solution)/shard_map/ppermute | solution.py:51
  217.3 49.4 %collective-permute-start.36 = (bf16[256,2048]{1,0:T(8,128)(2,1)S(1)}, bf16[256,2048]{1,0:T(8,128)(2,1)S(1)}, u32[]{:S(2)}, u32[]{:S(2)}) collective-permute-start(bf16[256,2048]{1,0:T(8,128)(2,1)S(1)} %pad_maximum_fusion.1), channel_id=1, source_target_pairs={{0,2},{1,3},{2,0},{3,1},{4,6},{5,7},{6,4},{7,5},{8,10},{9,11},{10,... | collective-permute-start | bytes 3145736 | tf_op jit(solution)/shard_map/ppermute | solution.py:51
  222.2 44.6 %collective-permute-start.39 = (bf16[256,2048]{1,0:T(8,128)(2,1)S(1)}, bf16[256,2048]{1,0:T(8,128)(2,1)S(1)}, u32[]{:S(2)}, u32[]{:S(2)}) collective-permute-start(bf16[256,2048]{1,0:T(8,128)(2,1)S(1)} %pad_maximum_fusion.2), channel_id=1, source_target_pairs={{0,4},{1,5},{2,6},{3,7},{4,0},{5,1},{6,2},{7,3},{8,12},{9,13},{10,... | collective-permute-start | bytes 3145736 | tf_op jit(solution)/shard_map/ppermute | solution.py:51
  246.0 36.7 %collective-permute-start.29 = (bf16[352,2048]{1,0:T(8,128)(2,1)}, bf16[352,2048]{1,0:T(8,128)(2,1)}, u32[]{:S(2)}, u32[]{:S(2)}) collective-permute-start(bf16[352,2048]{1,0:T(8,128)(2,1)} %get-tuple-element.289), channel_id=1, source_target_pairs={{0,8},{24,16},{1,9},{25,17},{2,10},{26,18},{3,11},{27,19},{4,12},{... | collective-permute-start | bytes 4325384 | tf_op jit(solution)/shard_map/ppermute | solution.py:335
  270.4 35.8 %collective-permute-start.40 = (bf16[256,2048]{1,0:T(8,128)(2,1)}, bf16[256,2048]{1,0:T(8,128)(2,1)}, u32[]{:S(2)}, u32[]{:S(2)}) collective-permute-start(bf16[256,2048]{1,0:T(8,128)(2,1)} %bitcast.22.g0_ref), channel_id=1, source_target_pairs={{0,4},{1,5},{2,6},{3,7},{4,0},{5,1},{6,2},{7,3},{8,12},{9,13},{10,... | collective-permute-start | bytes 3145736 | tf_op jit(solution)/shard_map/ppermute | solution.py:51
  271.9 34.2 %collective-permute-start.41 = (bf16[256,2048]{1,0:T(8,128)(2,1)}, bf16[256,2048]{1,0:T(8,128)(2,1)}, u32[]{:S(2)}, u32[]{:S(2)}) collective-permute-start(bf16[256,2048]{1,0:T(8,128)(2,1)} %bitcast.22.g0_ref), channel_id=1, source_target_pairs={{0,1},{1,0},{2,3},{3,2},{4,5},{5,4},{6,7},{7,6},{8,9},{9,8},{10,11... | collective-permute-start | bytes 3145736 | tf_op jit(solution)/shard_map/ppermute | solution.py:51
  330.3 35.9 %collective-permute-start.42 = (bf16[352,2048]{1,0:T(8,128)(2,1)}, bf16[352,2048]{1,0:T(8,128)(2,1)}, u32[]{:S(2)}, u32[]{:S(2)}) collective-permute-start(bf16[352,2048]{1,0:T(8,128)(2,1)} %get-tuple-element.430), channel_id=1, source_target_pairs={{0,8},{8,0},{16,24},{24,16},{1,9},{9,1},{17,25},{25,17},{2,10},{10... | collective-permute-start | bytes 4325384 | tf_op jit(solution)/shard_map/ppermute | solution.py:331
  357.9 47.1 %collective-permute-start.48 = (bf16[256,2048]{1,0:T(8,128)(2,1)}, bf16[256,2048]{1,0:T(8,128)(2,1)S(1)}, u32[]{:S(2)}, u32[]{:S(2)}) collective-permute-start(bf16[256,2048]{1,0:T(8,128)(2,1)} %fusion.61), channel_id=1, source_target_pairs={{0,4},{1,5},{2,6},{3,7},{4,0},{5,1},{6,2},{7,3},{8,12},{9,13},{10,... | collective-permute-start | bytes 3145736 | tf_op jit(solution)/shard_map/ppermute | solution.py:51
  394.2 35.2 %collective-permute-start.46 = (bf16[352,2048]{1,0:T(8,128)(2,1)S(1)}, bf16[352,2048]{1,0:T(8,128)(2,1)S(1)}, u32[]{:S(2)}, u32[]{:S(2)}) collective-permute-start(bf16[352,2048]{1,0:T(8,128)(2,1)S(1)} %get-tuple-element.428), channel_id=1, source_target_pairs={{0,8},{8,0},{16,24},{24,16},{1,9},{9,1},{17,25},{25,17},{2,10},{10... | collective-permute-start | bytes 4325384 | tf_op jit(solution)/shard_map/ppermute | solution.py:331
  433.4 36.6 %collective-permute-start.55 = (bf16[352,2048]{1,0:T(8,128)(2,1)S(1)}, bf16[352,2048]{1,0:T(8,128)(2,1)S(1)}, u32[]{:S(2)}, u32[]{:S(2)}) collective-permute-start(bf16[352,2048]{1,0:T(8,128)(2,1)S(1)} %get-tuple-element.426), channel_id=1, source_target_pairs={{0,8},{8,0},{16,24},{24,16},{1,9},{9,1},{17,25},{25,17},{2,10},{10... | collective-permute-start | bytes 4325384 | tf_op jit(solution)/shard_map/ppermute | solution.py:331
  453.0 43.8 %collective-permute-start.54 = (bf16[256,2048]{1,0:T(8,128)(2,1)}, bf16[256,2048]{1,0:T(8,128)(2,1)}, u32[]{:S(2)}, u32[]{:S(2)}) collective-permute-start(bf16[256,2048]{1,0:T(8,128)(2,1)} %slice.288), channel_id=1, source_target_pairs={{0,2},{1,3},{2,0},{3,1},{4,6},{5,7},{6,4},{7,5},{8,10},{9,11},{10,... | collective-permute-start | bytes 3145736 | tf_op jit(solution)/shard_map/ppermute | solution.py:51
  471.6 37.0 %collective-permute-start.62 = (bf16[352,2048]{1,0:T(8,128)(2,1)}, bf16[352,2048]{1,0:T(8,128)(2,1)}, u32[]{:S(2)}, u32[]{:S(2)}) collective-permute-start(bf16[352,2048]{1,0:T(8,128)(2,1)} %add_convert_fusion.2), channel_id=1, source_target_pairs={{8,0},{16,24},{9,1},{17,25},{10,2},{18,26},{11,3},{19,27},{12,4},{... | collective-permute-start | bytes 4325384 | tf_op jit(solution)/shard_map/ppermute | solution.py:336
  474.7 34.0 %collective-permute-start.61 = (bf16[352,2048]{1,0:T(8,128)(2,1)}, bf16[352,2048]{1,0:T(8,128)(2,1)}, u32[]{:S(2)}, u32[]{:S(2)}) collective-permute-start(bf16[352,2048]{1,0:T(8,128)(2,1)} %add_convert_fusion.3), channel_id=1, source_target_pairs={{8,16},{16,8},{9,17},{17,9},{10,18},{18,10},{11,19},{19,11},{12,20... | collective-permute-start | bytes 4325384 | tf_op jit(solution)/shard_map/ppermute | solution.py:337
  511.0 38.2 %collective-permute-start.74 = (bf16[352,2048]{1,0:T(8,128)(2,1)S(1)}, bf16[352,2048]{1,0:T(8,128)(2,1)S(1)}, u32[]{:S(2)}, u32[]{:S(2)}) collective-permute-start(bf16[352,2048]{1,0:T(8,128)(2,1)S(1)} %add_convert_fusion.1), channel_id=1, source_target_pairs={{8,0},{16,24},{9,1},{17,25},{10,2},{18,26},{11,3},{19,27},{12,4},{... | collective-permute-start | bytes 4325384 | tf_op jit(solution)/shard_map/ppermute | solution.py:336
  513.0 35.0 %collective-permute-start.73 = (bf16[256,2048]{1,0:T(8,128)(2,1)S(1)}, bf16[256,2048]{1,0:T(8,128)(2,1)S(1)}, u32[]{:S(2)}, u32[]{:S(2)}) collective-permute-start(bf16[256,2048]{1,0:T(8,128)(2,1)S(1)} %add_convert_fusion.16), channel_id=1, source_target_pairs={{8,16},{16,8},{9,17},{17,9},{10,18},{18,10},{11,19},{19,11},{12,20... | collective-permute-start | bytes 3145736 | tf_op jit(solution)/shard_map/ppermute | solution.py:337
  513.8 35.3 %collective-permute-start.71 = (bf16[256,2048]{1,0:T(8,128)(2,1)S(1)}, bf16[256,2048]{1,0:T(8,128)(2,1)S(1)}, u32[]{:S(2)}, u32[]{:S(2)}) collective-permute-start(bf16[256,2048]{1,0:T(8,128)(2,1)S(1)} %add_convert_fusion.19), channel_id=1, source_target_pairs={{0,8},{24,16},{1,9},{25,17},{2,10},{26,18},{3,11},{27,19},{4,12},{... | collective-permute-start | bytes 3145736 | tf_op jit(solution)/shard_map/ppermute | solution.py:335
  560.2 54.2 %collective-permute-start.70 = (bf16[256,2048]{1,0:T(8,128)(2,1)S(1)}, bf16[256,2048]{1,0:T(8,128)(2,1)S(1)}, u32[]{:S(2)}, u32[]{:S(2)}) collective-permute-start(bf16[256,2048]{1,0:T(8,128)(2,1)S(1)} %pad_maximum_fusion.4), channel_id=1, source_target_pairs={{0,4},{1,5},{2,6},{3,7},{4,0},{5,1},{6,2},{7,3},{8,12},{9,13},{10,... | collective-permute-start | bytes 3145736 | tf_op jit(solution)/shard_map/ppermute | solution.py:51
  562.6 51.7 %collective-permute-start.64 = (bf16[256,2048]{1,0:T(8,128)(2,1)S(1)}, bf16[256,2048]{1,0:T(8,128)(2,1)S(1)}, u32[]{:S(2)}, u32[]{:S(2)}) collective-permute-start(bf16[256,2048]{1,0:T(8,128)(2,1)S(1)} %convolution_convert_fusion.8), channel_id=1, source_target_pairs={{0,1},{1,0},{2,3},{3,2},{4,5},{5,4},{6,7},{7,6},{8,9},{9,8},{10,11... | collective-permute-start | bytes 3145736 | tf_op jit(solution)/shard_map/ppermute | solution.py:51
  575.6 38.8 %collective-permute-start.67 = (bf16[256,2048]{1,0:T(8,128)(2,1)S(1)}, bf16[256,2048]{1,0:T(8,128)(2,1)S(1)}, u32[]{:S(2)}, u32[]{:S(2)}) collective-permute-start(bf16[256,2048]{1,0:T(8,128)(2,1)S(1)} %pad_maximum_fusion.3), channel_id=1, source_target_pairs={{0,2},{1,3},{2,0},{3,1},{4,6},{5,7},{6,4},{7,5},{8,10},{9,11},{10,... | collective-permute-start | bytes 3145736 | tf_op jit(solution)/shard_map/ppermute | solution.py:51
  (196 other events, 2234.1 us)
Sparse Core Ops, SparseCore 0:
  24.7 28.2 all-gather.1
